TPU v7x, 128 devices: a whole 4x4x4 slice. The times are simulated.
128 devices in a mesh: group: 4 (over z), table: 32 (over y, x, core).
Axes of the slice: x: 4, y: 4, z: 4, core: 2. Of those that a mesh axis runs over, the one named last changes fastest.
Arguments:
- table: float32 [128, 2048, 128], P('table'), may hold values from -0.36 to 0.36
- accum: float32 [128, 2048], P('table'), may hold values from 0.05 to 2
- w_hidden: bfloat16 [128, 128, 128], replicated, may hold values from -0.5 to 0.5
- w_out: float32 [128], replicated, may hold values from -1.8 to 1.8
- ids: int32 [128, 8, 16384], P('table', None, 'group'), may hold values from 0 to 2047, as said below
- labels: float32 [16384], P(('group', 'table')), may hold values from 0 to 1, as said below
- touched: int32 [128, 512], P('table'), may hold values from 0 to 2047, as said below
- row_noise: float32 [128, 512, 128], P('table'), may hold values from -1.8 to 1.8
- dense_noise: float32 [128, 128, 128], P('table', 'group'), may hold values from -3.6 to 3.6
Outputs:
- new_table: float32 [128, 2048, 128], P('table')
- new_accum: float32 [128, 2048], P('table')
- dense_grad: float32 [128, 128, 128], P('table', 'group')
Inputs may be any that keep to these rules, and one draw needn't show every extreme that they name: `touched`: for each feature, 512 different rows of that feature's table. `ids`: every id of feature f is one of the rows listed for f in touched. `labels`: each target is 0 or 1.
All inputs are finite; a program needn't handle non-finite values.
Results may differ from a plain program's by a relative error of at most 0.003.
Values may be sent and summed in bfloat16 or wider, within the bound.
A program may use at most 128 MiB of HBM per device.

v0:
```python
import math

import jax
import jax.numpy as jnp
from jax import lax
from jax.sharding import PartitionSpec as P

CLIP = 1.0
LEARN = 0.05


def silu_slope(pre):
    gate = jax.nn.sigmoid(pre)
    return gate * (1.0 + pre * (1.0 - gate))


def pick_rows(source, where):
    return source[where]


def put_rows(target, where, values):
    return target.at[where].set(values)


def count_hits(ids, start, block, rows_f):
    bags = lax.dynamic_slice_in_dim(ids, start, block, 2)
    slots = lax.broadcasted_iota(jnp.int32, (1, 1, rows_f), 2)
    total = jnp.zeros((ids.shape[0], block, rows_f), jnp.bfloat16)
    for position in range(ids.shape[1]):
        total = total + (bags[:, position, :, None] == slots).astype(jnp.bfloat16)
    return total


def body(table, accum, w_hidden, w_out, ids, labels, touched, row_noise, dense_noise):
    f_dev, rows_f, width = table.shape
    b_group = ids.shape[2]
    b_dev = labels.shape[0]
    features = w_hidden.shape[0]
    hidden = w_hidden.shape[2]
    block = math.gcd(b_group, 512)
    block_count = b_group // block
    offset = lax.axis_index("table") * b_dev
    table_low = table.astype(jnp.bfloat16)

    def pool_block(number):
        counts = count_hits(ids, number * block, block, rows_f)
        return jnp.einsum("fbr,fre->bfe", counts, table_low, preferred_element_type=jnp.float32)

    pooled = lax.map(pool_block, jnp.arange(block_count, dtype=jnp.int32))
    pooled = pooled.reshape(b_group, f_dev, width).astype(jnp.bfloat16)
    repeats = jnp.sum((ids[:, :, None, :] == ids[:, None, :, :]).astype(jnp.float32), axis=(1, 2))
    gathered = lax.all_to_all(pooled, "table", split_axis=0, concat_axis=1, tiled=True)
    flat = gathered.reshape(b_dev, features * width)
    w_flat = w_hidden.reshape(features * width, hidden)
    pre = jnp.dot(flat, w_flat, preferred_element_type=jnp.float32)
    logit = jnp.sum(jax.nn.silu(pre) * w_out, axis=1)
    prob = jax.nn.sigmoid(logit)
    delta = silu_slope(pre) * w_out * (prob - labels)[:, None]
    delta_low = delta.astype(jnp.bfloat16)
    grad_pool = lax.dot_general(
        delta_low, w_flat, (((1,), (1,)), ((), ())), preferred_element_type=jnp.float32
    )
    grad_pool = grad_pool.astype(jnp.bfloat16).reshape(b_dev, features, width)
    dense_sq = jnp.sum(jnp.square(flat.astype(jnp.float32)), axis=1) * jnp.sum(
        delta * delta, axis=1
    )
    returned = lax.all_to_all(grad_pool, "table", split_axis=1, concat_axis=0, tiled=True)
    grad_sq = jnp.sum(jnp.square(returned.astype(jnp.float32)), axis=2)
    embed_part = jnp.sum(repeats.T * grad_sq, axis=1)
    dense_part = lax.dynamic_update_slice_in_dim(
        jnp.zeros((b_group,), jnp.float32), dense_sq, offset, 0
    )
    totals = lax.psum(embed_part + dense_part, "table")
    factor_all = CLIP / jnp.maximum(jnp.sqrt(totals), CLIP)
    factor_own = lax.dynamic_slice_in_dim(factor_all, offset, b_dev, 0)
    arrived = (factor_all[:, None, None] * returned.astype(jnp.float32)).astype(jnp.bfloat16)
    clip_rows = (factor_own[:, None] * delta).astype(jnp.bfloat16)
    group_sum = lax.psum_scatter(
        jnp.einsum("bfe,bh->feh", gathered, clip_rows, preferred_element_type=jnp.float32).astype(
            jnp.bfloat16
        ),
        "table",
        scatter_dimension=0,
        tiled=True,
    )
    dense_sum = lax.psum_scatter(group_sum, "group", scatter_dimension=1, tiled=True).astype(
        jnp.float32
    )
    dense_grad = dense_sum + dense_noise

    def add_block(number, total):
        counts = count_hits(ids, number * block, block, rows_f)
        rows_now = lax.dynamic_slice_in_dim(arrived, number * block, block, 0)
        return total + jnp.einsum(
            "fbr,bfe->fre", counts, rows_now, preferred_element_type=jnp.float32
        )

    grads = lax.fori_loop(0, block_count, add_block, jnp.zeros((f_dev, rows_f, width), jnp.float32))
    summed = lax.psum(grads.astype(jnp.bfloat16), "group").astype(jnp.float32)
    listed = jax.vmap(pick_rows)(summed, touched)
    listed = listed + row_noise
    new_acc = jax.vmap(pick_rows)(accum, touched) + jnp.mean(listed * listed, axis=2)
    new_rows = jax.vmap(pick_rows)(table, touched) - LEARN * listed / jnp.sqrt(new_acc)[:, :, None]
    new_table = jax.vmap(put_rows)(table, touched, new_rows)
    new_accum = jax.vmap(put_rows)(accum, touched, new_acc)
    return (new_table, new_accum, dense_grad)


def solution(mesh):
    in_specs = (
        P("table", None, None),
        P("table", None),
        P(),
        P(),
        P("table", None, "group"),
        P(("group", "table")),
        P("table", None),
        P("table", None, None),
        P("table", "group", None),
    )
    out_specs = (P("table", None, None), P("table", None), P("table", "group", None))
    return jax.shard_map(body, mesh=mesh, in_specs=in_specs, out_specs=out_specs, check_vma=False)
```

profile of v0, /device:TPU:0, one launch (start us, length us, event | category | flops | bytes accessed | tf_op | source)
XLA Modules:
  0.0 748.0 jit_solution(10196888664727080277)
XLA Ops:
  8.0 4.5 copy.90
  12.5 0.3 copy.50
  12.9 2.5 convert_element_type.139
  15.4 175.4 %while.24 = (s32[]{:T(128)}, bf16[8,512,4,128]{3,1,0,2:T(8,128)(2,1)}, s32[8]{0:T(128)S(1)}, s32[4,8,4096]{2,0,1:T(4,128)S(1)}, bf16[4,2048,128]{2,1,0:T(8,128)(...) while((s32[]{:T(128)}, ...), condition=%wide.region_2.3_spmd, body=%wide.region_1.2_spmd.sunk | while | flops 1207959552 | bytes 3342671 | solution.py:49
  15.4 0.6 dynamic_slice.31
  16.6 20.6 %fusion.96 = bf16[8,512,4,128]{3,1,0,2:T(8,128)(2,1)} fusion(bf16[8,512,4,128]{3,1,0,2:T(8,128)(2,1)} %get-tuple-element.314, s32[]{:T(128)S(6)} %copy.75, bf16[4,2048,128]{2,1,0:T(8,128)(2,1)S(1)} %get-tuple-element.333, s32[4,512]{1,0:T(4,128)S(1)} %get-tuple-element.277, s32[4,512]{1,0:T(4,128)S(1)} %get-tuple-element.278, ...), kind=kOutput, calls=%fused_computation.38.clone.1 | convolution fusion | flops 1207959552 | bytes 3211268 | tf_op jit(solution)/shard_map/while/body/eval_jaxpr/fbr,fre->bfe/dot_general | solution.py:47
  37.3 0.6 dynamic_slice.31
  38.6 20.7 %fusion.96 = bf16[8,512,4,128]{3,1,0,2:T(8,128)(2,1)} fusion(bf16[8,512,4,128]{3,1,0,2:T(8,128)(2,1)} %get-tuple-element.314, s32[]{:T(128)S(6)} %copy.75, bf16[4,2048,128]{2,1,0:T(8,128)(2,1)S(1)} %get-tuple-element.333, s32[4,512]{1,0:T(4,128)S(1)} %get-tuple-element.277, s32[4,512]{1,0:T(4,128)S(1)} %get-tuple-element.278, ...), kind=kOutput, calls=%fused_computation.38.clone.1 | convolution fusion | flops 1207959552 | bytes 3211268 | tf_op jit(solution)/shard_map/while/body/eval_jaxpr/fbr,fre->bfe/dot_general | solution.py:47
  59.2 0.6 dynamic_slice.31
  60.5 20.7 %fusion.96 = bf16[8,512,4,128]{3,1,0,2:T(8,128)(2,1)} fusion(bf16[8,512,4,128]{3,1,0,2:T(8,128)(2,1)} %get-tuple-element.314, s32[]{:T(128)S(6)} %copy.75, bf16[4,2048,128]{2,1,0:T(8,128)(2,1)S(1)} %get-tuple-element.333, s32[4,512]{1,0:T(4,128)S(1)} %get-tuple-element.277, s32[4,512]{1,0:T(4,128)S(1)} %get-tuple-element.278, ...), kind=kOutput, calls=%fused_computation.38.clone.1 | convolution fusion | flops 1207959552 | bytes 3211268 | tf_op jit(solution)/shard_map/while/body/eval_jaxpr/fbr,fre->bfe/dot_general | solution.py:47
  81.2 0.6 dynamic_slice.31
  82.4 20.6 %fusion.96 = bf16[8,512,4,128]{3,1,0,2:T(8,128)(2,1)} fusion(bf16[8,512,4,128]{3,1,0,2:T(8,128)(2,1)} %get-tuple-element.314, s32[]{:T(128)S(6)} %copy.75, bf16[4,2048,128]{2,1,0:T(8,128)(2,1)S(1)} %get-tuple-element.333, s32[4,512]{1,0:T(4,128)S(1)} %get-tuple-element.277, s32[4,512]{1,0:T(4,128)S(1)} %get-tuple-element.278, ...), kind=kOutput, calls=%fused_computation.38.clone.1 | convolution fusion | flops 1207959552 | bytes 3211268 | tf_op jit(solution)/shard_map/while/body/eval_jaxpr/fbr,fre->bfe/dot_general | solution.py:47
  103.1 0.6 dynamic_slice.31
  104.4 20.6 %fusion.96 = bf16[8,512,4,128]{3,1,0,2:T(8,128)(2,1)} fusion(bf16[8,512,4,128]{3,1,0,2:T(8,128)(2,1)} %get-tuple-element.314, s32[]{:T(128)S(6)} %copy.75, bf16[4,2048,128]{2,1,0:T(8,128)(2,1)S(1)} %get-tuple-element.333, s32[4,512]{1,0:T(4,128)S(1)} %get-tuple-element.277, s32[4,512]{1,0:T(4,128)S(1)} %get-tuple-element.278, ...), kind=kOutput, calls=%fused_computation.38.clone.1 | convolution fusion | flops 1207959552 | bytes 3211268 | tf_op jit(solution)/shard_map/while/body/eval_jaxpr/fbr,fre->bfe/dot_general | solution.py:47
  125.0 0.6 dynamic_slice.31
  126.3 20.7 %fusion.96 = bf16[8,512,4,128]{3,1,0,2:T(8,128)(2,1)} fusion(bf16[8,512,4,128]{3,1,0,2:T(8,128)(2,1)} %get-tuple-element.314, s32[]{:T(128)S(6)} %copy.75, bf16[4,2048,128]{2,1,0:T(8,128)(2,1)S(1)} %get-tuple-element.333, s32[4,512]{1,0:T(4,128)S(1)} %get-tuple-element.277, s32[4,512]{1,0:T(4,128)S(1)} %get-tuple-element.278, ...), kind=kOutput, calls=%fused_computation.38.clone.1 | convolution fusion | flops 1207959552 | bytes 3211268 | tf_op jit(solution)/shard_map/while/body/eval_jaxpr/fbr,fre->bfe/dot_general | solution.py:47
  146.9 0.6 dynamic_slice.31
  148.2 20.7 %fusion.96 = bf16[8,512,4,128]{3,1,0,2:T(8,128)(2,1)} fusion(bf16[8,512,4,128]{3,1,0,2:T(8,128)(2,1)} %get-tuple-element.314, s32[]{:T(128)S(6)} %copy.75, bf16[4,2048,128]{2,1,0:T(8,128)(2,1)S(1)} %get-tuple-element.333, s32[4,512]{1,0:T(4,128)S(1)} %get-tuple-element.277, s32[4,512]{1,0:T(4,128)S(1)} %get-tuple-element.278, ...), kind=kOutput, calls=%fused_computation.38.clone.1 | convolution fusion | flops 1207959552 | bytes 3211268 | tf_op jit(solution)/shard_map/while/body/eval_jaxpr/fbr,fre->bfe/dot_general | solution.py:47
  168.9 0.6 dynamic_slice.31
  170.1 20.6 %fusion.96 = bf16[8,512,4,128]{3,1,0,2:T(8,128)(2,1)} fusion(bf16[8,512,4,128]{3,1,0,2:T(8,128)(2,1)} %get-tuple-element.314, s32[]{:T(128)S(6)} %copy.75, bf16[4,2048,128]{2,1,0:T(8,128)(2,1)S(1)} %get-tuple-element.333, s32[4,512]{1,0:T(4,128)S(1)} %get-tuple-element.277, s32[4,512]{1,0:T(4,128)S(1)} %get-tuple-element.278, ...), kind=kOutput, calls=%fused_computation.38.clone.1 | convolution fusion | flops 1207959552 | bytes 3211268 | tf_op jit(solution)/shard_map/while/body/eval_jaxpr/fbr,fre->bfe/dot_general | solution.py:47
  190.8 5.8 copy.43
  196.6 58.2 %all_to_all.27 = bf16[4096,4,128]{2,1,0:T(4,128)(2,1)S(1)} all-to-all(bf16[4096,4,128]{2,1,0:T(4,128)(2,1)S(1)} %copy.43), channel_id=1, replica_groups=mesh['group'=4,'table'=32] {'table'}, dimensions={0} | all-to-all | bytes 8388608 | tf_op jit(solution)/shard_map/all_to_all | solution.py:52
  254.8 2.5 copy.44
  257.3 6.4 copy.45
  263.8 5.0 multiply_reduce_fusion.4
  268.8 1.4 fusion.75
  270.1 3.1 copy.71
  273.3 4.9 all-to-all-start.1
  278.1 0.2 all-reduce.2.cloned.1.call-start
  278.4 0.6 convert_reduce_fusion
  279.0 0.1 multiply_reduce_fusion.3
  279.1 3.1 multiply_reduce_fusion
  282.3 49.4 %all-to-all-done.1 = bf16[128,128,128]{2,0,1:T(8,128)(2,1)} async-done(((bf16[128,128,128]{2,0,1:T(8,128)(2,1)}), bf16[128,128,128]{2,0,1:T(8,128)(2,1)}, u32[]{:S(2)}, u32[]{:S(2)}) %all-to-all-start.1) | async-done | bytes 4194336 | tf_op jit(solution)/shard_map/all_to_all | solution.py:67
  331.6 4.4 multiply_reduce_fusion.1
  336.1 0.2 add_dynamic-update-slice_fusion
  336.3 124.3 %psum.14 = f32[4096]{0:T(1024)S(1)} all-reduce(f32[4096]{0:T(1024)S(1)} %add_dynamic-update-slice_fusion), channel_id=1, replica_groups=mesh['group'=4,'table'=32] {'table'}, use_global_device_ids=true, to_apply=%region_8.9 | all-reduce | flops 4096 | bytes 32768 | tf_op jit(solution)/shard_map/psum | solution.py:73
  460.6 3.2 convert_element_type.144
  463.8 1.1 copy.49
  464.9 2.9 fusion.74
  467.9 156.8 %while.25 = (s32[]{:T(128)}, f32[4,2048,128]{2,1,0:T(8,128)}, s32[4,8,4096]{2,0,1:T(4,128)S(1)}, bf16[4096,4,128]{2,0,1:T(8,128)(2,1)}, s32[]{:T(128)}, /*index=...) while((s32[]{:T(128)}, f32[4,2048,128]{2,1,0:T(8,128)}, ...), condition=%wide.region_10.11_spmd.clone, body=%wide.region_9.10_spmd.clone.sunk | while | flops 1210056704 | bytes 9109829 | solution.py:98
  467.9 19.3 %select_add_fusion.2 = f32[4,2048,128]{2,1,0:T(8,128)} fusion(f32[4,2048,128]{2,1,0:T(8,128)} %get-tuple-element.361, s32[4,512]{1,0:T(4,128)S(1)} %get-tuple-element.289, s32[4,512]{1,0:T(4,128)S(1)} %get-tuple-element.290, s32[4,512]{1,0:T(4,128)S(1)} %get-tuple-element.291, s32[4,512]{1,0:T(4,128)S(1)} %get-tuple-element.292, ...), kind=kOutput, calls=%fused_computation.79.clone.1 | convolution fusion | flops 1210056704 | bytes 8978437 | tf_op jit(solution)/shard_map/while/body/eval_jaxpr/fbr,bfe->fre/dot_general | solution.py:94
  487.2 19.6 %select_add_fusion.2 = f32[4,2048,128]{2,1,0:T(8,128)} fusion(f32[4,2048,128]{2,1,0:T(8,128)} %get-tuple-element.361, s32[4,512]{1,0:T(4,128)S(1)} %get-tuple-element.289, s32[4,512]{1,0:T(4,128)S(1)} %get-tuple-element.290, s32[4,512]{1,0:T(4,128)S(1)} %get-tuple-element.291, s32[4,512]{1,0:T(4,128)S(1)} %get-tuple-element.292, ...), kind=kOutput, calls=%fused_computation.79.clone.1 | convolution fusion | flops 1210056704 | bytes 8978437 | tf_op jit(solution)/shard_map/while/body/eval_jaxpr/fbr,bfe->fre/dot_general | solution.py:94
  506.9 19.6 %select_add_fusion.2 = f32[4,2048,128]{2,1,0:T(8,128)} fusion(f32[4,2048,128]{2,1,0:T(8,128)} %get-tuple-element.361, s32[4,512]{1,0:T(4,128)S(1)} %get-tuple-element.289, s32[4,512]{1,0:T(4,128)S(1)} %get-tuple-element.290, s32[4,512]{1,0:T(4,128)S(1)} %get-tuple-element.291, s32[4,512]{1,0:T(4,128)S(1)} %get-tuple-element.292, ...), kind=kOutput, calls=%fused_computation.79.clone.1 | convolution fusion | flops 1210056704 | bytes 8978437 | tf_op jit(solution)/shard_map/while/body/eval_jaxpr/fbr,bfe->fre/dot_general | solution.py:94
  526.5 19.6 %select_add_fusion.2 = f32[4,2048,128]{2,1,0:T(8,128)} fusion(f32[4,2048,128]{2,1,0:T(8,128)} %get-tuple-element.361, s32[4,512]{1,0:T(4,128)S(1)} %get-tuple-element.289, s32[4,512]{1,0:T(4,128)S(1)} %get-tuple-element.290, s32[4,512]{1,0:T(4,128)S(1)} %get-tuple-element.291, s32[4,512]{1,0:T(4,128)S(1)} %get-tuple-element.292, ...), kind=kOutput, calls=%fused_computation.79.clone.1 | convolution fusion | flops 1210056704 | bytes 8978437 | tf_op jit(solution)/shard_map/while/body/eval_jaxpr/fbr,bfe->fre/dot_general | solution.py:94
  546.1 19.6 %select_add_fusion.2 = f32[4,2048,128]{2,1,0:T(8,128)} fusion(f32[4,2048,128]{2,1,0:T(8,128)} %get-tuple-element.361, s32[4,512]{1,0:T(4,128)S(1)} %get-tuple-element.289, s32[4,512]{1,0:T(4,128)S(1)} %get-tuple-element.290, s32[4,512]{1,0:T(4,128)S(1)} %get-tuple-element.291, s32[4,512]{1,0:T(4,128)S(1)} %get-tuple-element.292, ...), kind=kOutput, calls=%fused_computation.79.clone.1 | convolution fusion | flops 1210056704 | bytes 8978437 | tf_op jit(solution)/shard_map/while/body/eval_jaxpr/fbr,bfe->fre/dot_general | solution.py:94
  565.8 19.6 %select_add_fusion.2 = f32[4,2048,128]{2,1,0:T(8,128)} fusion(f32[4,2048,128]{2,1,0:T(8,128)} %get-tuple-element.361, s32[4,512]{1,0:T(4,128)S(1)} %get-tuple-element.289, s32[4,512]{1,0:T(4,128)S(1)} %get-tuple-element.290, s32[4,512]{1,0:T(4,128)S(1)} %get-tuple-element.291, s32[4,512]{1,0:T(4,128)S(1)} %get-tuple-element.292, ...), kind=kOutput, calls=%fused_computation.79.clone.1 | convolution fusion | flops 1210056704 | bytes 8978437 | tf_op jit(solution)/shard_map/while/body/eval_jaxpr/fbr,bfe->fre/dot_general | solution.py:94
  585.4 19.6 %select_add_fusion.2 = f32[4,2048,128]{2,1,0:T(8,128)} fusion(f32[4,2048,128]{2,1,0:T(8,128)} %get-tuple-element.361, s32[4,512]{1,0:T(4,128)S(1)} %get-tuple-element.289, s32[4,512]{1,0:T(4,128)S(1)} %get-tuple-element.290, s32[4,512]{1,0:T(4,128)S(1)} %get-tuple-element.291, s32[4,512]{1,0:T(4,128)S(1)} %get-tuple-element.292, ...), kind=kOutput, calls=%fused_computation.79.clone.1 | convolution fusion | flops 1210056704 | bytes 8978437 | tf_op jit(solution)/shard_map/while/body/eval_jaxpr/fbr,bfe->fre/dot_general | solution.py:94
  605.1 19.6 %select_add_fusion.2 = f32[4,2048,128]{2,1,0:T(8,128)} fusion(f32[4,2048,128]{2,1,0:T(8,128)} %get-tuple-element.361, s32[4,512]{1,0:T(4,128)S(1)} %get-tuple-element.289, s32[4,512]{1,0:T(4,128)S(1)} %get-tuple-element.290, s32[4,512]{1,0:T(4,128)S(1)} %get-tuple-element.291, s32[4,512]{1,0:T(4,128)S(1)} %get-tuple-element.292, ...), kind=kOutput, calls=%fused_computation.79.clone.1 | convolution fusion | flops 1210056704 | bytes 8978437 | tf_op jit(solution)/shard_map/while/body/eval_jaxpr/fbr,bfe->fre/dot_general | solution.py:94
  624.7 3.8 convert_element_type.151
  628.5 0.3 reduce-scatter.3.cloned.1.call-start
  628.9 5.5 convolution_convert_fusion.1
  634.6 0.1 and_reduce_fusion
  634.7 23.3 %gather_fusion = f32[2048,128]{1,0:T(8,128)S(1)} fusion(f32[4,2048,128]{2,1,0:T(8,128)} %copy.90, s32[2048]{0:T(1024)S(1)} %bitcast.113), kind=kCustom, calls=%fused_computation | custom fusion | bytes 2113536 | tf_op jit(solution)/shard_map/vmap()/gather | solution.py:18
  658.0 17.7 %gather_fusion.2 = f32[2048]{0:T(1024)S(1)} fusion(f32[4,2048]{1,0:T(4,128)S(1)} %copy-done, s32[2048]{0:T(1024)S(1)} %bitcast.114), kind=kCustom, calls=%fused_computation.2 | custom fusion | bytes 32768 | tf_op jit(solution)/shard_map/vmap()/gather | solution.py:18
  675.8 9.2 %all-reduce.2.cloned.1.call-done = bf16[4,2048,128]{2,1,0:T(8,128)(2,1)} async-done(((bf16[4,2048,128]{2,1,0:T(8,128)(2,1)}), bf16[4,2048,128]{2,1,0:T(8,128)(2,1)}) %all-reduce.2.cloned.1.call-update) | async-done | bytes 2097168 | tf_op jit(solution)/shard_map/psum | solution.py:99
  685.0 3.8 convert_element_type.152
  688.8 20.7 %gather_fusion.1 = f32[2048,128]{1,0:T(8,128)S(1)} fusion(f32[4,2048,128]{2,1,0:T(8,128)} %convert_element_type.152, s32[2048]{0:T(1024)S(1)} %bitcast.115), kind=kCustom, calls=%fused_computation.1 | custom fusion | bytes 2113536 | tf_op jit(solution)/shard_map/vmap()/gather | solution.py:18
  709.5 0.4 multiply_reduce_fusion.2
  709.9 8.1 %scatter_fusion.1 = f32[8192]{0:T(1024)S(1)} fusion(f32[8192]{0:T(1024)S(1)} %bitcast.111, s32[2048]{0:T(1024)S(1)} %bitcast.131, f32[2048]{0:T(1024)S(1)} %bitcast.133), kind=kCustom, calls=%fused_computation.4 | custom fusion | bytes 32768
  718.0 0.6 reshape.67
  718.7 1.6 divide_subtract_fusion
  720.3 9.8 %scatter_fusion = f32[8192,128]{1,0:T(8,128)} fusion(f32[8192,128]{1,0:T(8,128)} %bitcast.116, s32[2048]{0:T(1024)S(1)} %bitcast.132, f32[2048,128]{1,0:T(8,128)S(1)} %bitcast.129), kind=kCustom, calls=%fused_computation.3 | custom fusion | bytes 3153920
  730.1 9.1 %reduce-scatter.5.cloned.1.call-done = bf16[4,32,128]{2,1,0:T(8,128)(2,1)} async-done(((bf16[4,128,128]{2,1,0:T(8,128)(2,1)}), bf16[4,32,128]{2,1,0:T(8,128)(2,1)}) %reduce-scatter.5.cloned.1.call-update) | async-done | bytes 32784 | tf_op jit(solution)/shard_map/reduce_scatter | solution.py:86
  739.2 1.4 convert_add_fusion
  (59 shorter events, 0.7 us)
Async XLA Ops:
  8.0 4.5 copy-start.2
  254.8 8.9 %copy-start.6 = (f32[128]{0:T(128)S(1)}, f32[128]{0:T(128)}, u32[]{:S(2)}) copy-start(f32[128]{0:T(128)} %param.16) | copy-start | bytes 1540
  257.3 11.4 %copy-start.9 = (f32[128]{0:T(128)S(1)}, f32[128]{0:T(128)}, u32[]{:S(2)}) copy-start(f32[128]{0:T(128)} %param.18) | copy-start | bytes 1540
  263.8 5.0 copy-start.1
  273.3 58.3 %all-to-all-start.1 = ((bf16[128,128,128]{2,0,1:T(8,128)(2,1)}), bf16[128,128,128]{2,0,1:T(8,128)(2,1)}, u32[]{:S(2)}, u32[]{:S(2)}) async-start(bf16[128,128,128]{2,0,1:T(8,128)(2,1)} %bitcast.125), calls=%async_computation.1 | async-start | bytes 8388608 | tf_op jit(solution)/shard_map/all_to_all | solution.py:67
  278.1 406.8 %all-reduce.2.cloned.1.call-start = ((), (), s32[]{:S(2)}) async-start(), calls=%async_computation.4 | async-start | bytes 4194304 | tf_op jit(solution)/shard_map/psum | solution.py:99
  628.5 6.0 copy-start.5
  628.5 6.0 copy-start.8
  628.5 6.1 copy-start.7
  628.5 90.1 %reduce-scatter.3.cloned.1.call-start = ((), (), s32[]{:S(2)}) async-start(), calls=%async_computation.5 | async-start | bytes 4325376 | tf_op jit(solution)/shard_map/reduce_scatter | solution.py:78
  634.4 23.6 %copy-start = (f32[4,2048]{1,0:T(4,128)S(1)}, f32[4,2048]{1,0:T(4,128)}, u32[]{:S(2)}) copy-start(f32[4,2048]{1,0:T(4,128)} %param.14) | copy-start | bytes 98308
  634.4 104.8 %reduce-scatter.5.cloned.1.call-start = ((), (), s32[]{:S(2)}) async-start(), calls=%async_computation.6 | async-start | bytes 163840 | tf_op jit(solution)/shard_map/reduce_scatter | solution.py:86
  675.8 33.7 %copy-start.3 = (f32[4,512,128]{2,1,0:T(8,128)S(1)}, f32[4,512,128]{2,1,0:T(8,128)}, u32[]{:S(2)}) copy-start(f32[4,512,128]{2,1,0:T(8,128)} %param.20) | copy-start | bytes 3145732
  720.3 18.9 %copy-start.4 = (f32[4,32,128]{2,1,0:T(8,128)S(1)}, f32[4,32,128]{2,1,0:T(8,128)}, u32[]{:S(2)}) copy-start(f32[4,32,128]{2,1,0:T(8,128)} %param.21) | copy-start | bytes 196612
Sparse Core Ops, SparseCore 0:
  628.7 56.2 all-reduce.1
  718.8 20.3 reduce-scatter.4
Sparse Core Ops, SparseCore 1:
  634.5 79.2 reduce-scatter.2
where the time goes:
time: 750 us; the launch traced here: 748 us
  matrix products  334 us (45%)
  blocking collectives  183 us (24%)
  local copies, waits for them, and re-layouts  109 us (15%)
  waiting for transfers between devices  67.8 us (9%)
  other arithmetic  28.4 us (4%)
  between operations  15.8 us (2%)
    dot_general x8, matrix products, pool_block(): jnp.einsum('fbr,fre->bfe', counts, table_low, preferred_element_type=jnp....  165 us
    dot_general x8, matrix products, add_block(): jnp.einsum('fbr,bfe->fre', counts, rows_now, preferred_element_type=jnp.f...  157 us
    psum x1, blocking collectives, body(): totals = lax.psum(embed_part + dense_part, 'table')  124 us
    gather x4, local copies, waits for them, and re-layouts, pick_rows(): return source[where]  61.7 us
    all_to_all x1, blocking collectives, body(): lax.all_to_all(pooled, 'table', split_axis=0, concat_axis=1, tiled=True)  58.2 us
    all_to_all x1, waiting for transfers between devices, body(): lax.all_to_all(grad_pool, 'table', split_axis=1, concat_axis=0, tiled=True)  49.4 us
    unnamed x28, local copies, waits for them, and re-layouts  22.8 us
  transfers between devices with their start and end apart: 4, of which 3 were waited for; matrix products, arithmetic and copies ran while one was open for 13% of the time, Pallas kernels for 0%

commit v1 on v0

v1 whole, which is shorter than its diff:
```python
import functools

import jax
import jax.numpy as jnp
from jax import lax
from jax.experimental import pallas as pl
from jax.experimental.pallas import tpu as pltpu
from jax.sharding import PartitionSpec as P

CLIP = 1.0
LEARN = 0.05
MESH = pl.DeviceIdType.MESH
BF = jnp.bfloat16
F32 = jnp.float32
LAG = 2


def code_of(ids):
    return lax.shift_left((ids & 127) + 128, lax.shift_right_logical(ids, 7)).astype(F32)


def split_dot(a, b, dims):
    return lax.dot_general(a, b, (dims, ((), ())), preferred_element_type=F32)


def core(
    touched_s, accum_s, ids, touched_v, w_out, labels, noise, table_h, w_h,
    rows_out, nacc_out, dense_out,
    table_v, w_v, trows, ttr, tcode, wtr, counts, pool, keep, stage, sibin, outb, slots,
    pacc, clip, accb, s_acc, zsend, zrecv, rg, dsend,
    load_sem, s1, r1, s2, r2, s3, r3, s4, r4, s5, r5, s6, r6, s7, r7,
):
    g = lax.axis_index("group")
    t = lax.axis_index("table")
    c = lax.rem(t, 2)
    p = t // 2
    y = p // 4
    x = lax.rem(p, 4)
    sib = t + 1 - 2 * c

    def ahead(off):
        return lax.rem(y + off // 4, 4) * 4 + lax.rem(x + lax.rem(off, 4), 4)

    def behind(off):
        return lax.rem(y + 4 - off // 4, 4) * 4 + lax.rem(x + 4 - lax.rem(off, 4), 4)

    load_table = pltpu.make_async_copy(table_h, table_v, load_sem.at[0])
    load_w = pltpu.make_async_copy(w_h, w_v, load_sem.at[1])
    load_table.start()
    load_w.start()

    barrier = pltpu.get_barrier_semaphore()

    def greet(off, carry):
        pl.semaphore_signal(
            barrier, inc=1, device_id=(g, ahead(off) * 2 + c), device_id_type=MESH
        )
        return carry

    lax.fori_loop(1, 16, greet, 0)
    pl.semaphore_signal(barrier, inc=1, device_id=(g, sib), device_id_type=MESH)
    for i in range(1, 4):
        pl.semaphore_signal(
            barrier, inc=1, device_id=(lax.rem(g + i, 4), t), device_id_type=MESH
        )

    for f in range(4):
        row = code_of(touched_v[f : f + 1, :])
        for q in range(4):
            wide = jnp.broadcast_to(row[:, q * 128 : (q + 1) * 128], (128, 128))
            tcode[f, q * 128 : (q + 1) * 128, :] = wide.T.astype(BF)

    load_table.wait()

    def pick(n, carry):
        f = n // 64
        k = lax.rem(n, 64) * 8
        for i in range(8):
            r = touched_s[f, k + i]
            trows[f, pl.ds(k + i, 1), :] = table_v[f, pl.ds(r, 1), :]
        return carry

    lax.fori_loop(0, 256, pick, 0)
    for f in range(4):
        ttr[f] = trows[f].T.astype(BF)

    load_w.wait()
    for f in range(4):
        wtr[:, f * 128 : (f + 1) * 128] = w_v[t * 4 + f].astype(F32).T.astype(BF)

    pl.semaphore_wait(barrier, 19)

    rows16 = lax.broadcasted_iota(jnp.int32, (16, 256), 0)

    def relay(s):
        pltpu.make_async_remote_copy(
            src_ref=stage.at[s], dst_ref=sibin.at[s], send_sem=s1.at[s], recv_sem=r1.at[s],
            device_id=(g, sib), device_id_type=MESH,
        ).wait_recv()
        outb[s] = (keep[s] + sibin[s].astype(F32)).astype(BF)

    def out_copy(s):
        return pltpu.make_async_remote_copy(
            src_ref=outb.at[s], dst_ref=slots.at[p], send_sem=s2.at[s], recv_sem=r2.at[p],
            device_id=(g, ahead(15 - s) * 2 + c), device_id_type=MESH,
        )

    def sib_copy(s):
        return pltpu.make_async_remote_copy(
            src_ref=stage.at[s], dst_ref=sibin.at[s], send_sem=s1.at[s], recv_sem=r1.at[s],
            device_id=(g, sib), device_id_type=MESH,
        )

    def step(s, carry):
        b0 = pl.multiple_of(ahead(15 - s) * 256, 256)

        def feature(f, carry):
            extra, sumsq = carry
            bag = ids[f, :, pl.ds(b0, 256)]
            code = code_of(bag)
            mult = jnp.ones((8, 256), F32)
            for d in range(1, 8):
                mult = mult + jnp.where(bag == pltpu.roll(bag, d, 0), 1.0, 0.0)
            repeats = jnp.sum(mult, axis=0, keepdims=True)
            extra = jnp.where(rows16 == c * 4 + f, repeats, extra)
            codes = []
            mults = []
            for half in range(2):
                lanes = slice(half * 128, half * 128 + 128)
                codes.append(
                    [jnp.broadcast_to(code[h : h + 1, lanes], (16, 128)).astype(BF) for h in range(8)]
                )
                mults.append(
                    [jnp.broadcast_to(mult[h : h + 1, lanes], (16, 128)).astype(BF) for h in range(8)]
                )
            total = jnp.zeros((128, 256), F32)
            zero = jnp.zeros((16, 128), BF)
            for part in range(2):
                tiles = []
                for kt in range(16):
                    k0 = part * 256 + kt * 16
                    want = tcode[f, k0 : k0 + 16, :]
                    both = []
                    for half in range(2):
                        count = zero
                        for h in range(8):
                            count = jnp.where(want == codes[half][h], mults[half][h], count)
                        both.append(count)
                    tiles.append(jnp.concatenate(both, axis=1))
                block = jnp.concatenate(tiles, axis=0)
                counts[f, part * 256 : part * 256 + 256, pl.ds(b0, 256)] = block
                total = total + split_dot(
                    ttr[f, :, part * 256 : part * 256 + 256], block, ((1,), (0,))
                )
            low = total.astype(BF)
            pool[pl.ds(pl.multiple_of(f * 128, 128), 128), :] = low
            wide = low.astype(F32)
            sumsq = sumsq + jnp.sum(wide * wide, axis=0, keepdims=True)
            return extra, sumsq

        extra, sumsq = lax.fori_loop(
            0, 4, feature, (jnp.zeros((16, 256), F32), jnp.zeros((1, 256), F32))
        )
        high = sumsq.astype(BF).astype(F32)
        extra = jnp.where(rows16 == 8 + 2 * c, high, extra)
        extra = jnp.where(rows16 == 9 + 2 * c, sumsq - high, extra)
        part = split_dot(wtr[...], pool[...], ((1,), (0,)))
        first = c == 0
        keep[s, 0:128, :] = jnp.where(first, part[:, :128], part[:, 128:])
        keep[s, 128:144, :] = jnp.where(first, extra[:, :128], extra[:, 128:])
        stage[s, 0:128, :] = jnp.where(first, part[:, 128:], part[:, :128]).astype(BF)
        stage[s, 128:144, :] = jnp.where(first, extra[:, 128:], extra[:, :128]).astype(BF)
        sib_copy(s).start()

        @pl.when(s >= LAG)
        def _():
            relay(s - LAG)
            out_copy(s - LAG).start()

        return carry

    lax.fori_loop(0, 16, step, 0)
    relay(14)
    out_copy(14).start()
    relay(15)
    slots[p] = outb[15]

    pacc[...] = slots[p, 0:128, :].astype(F32)

    def arrive(s, carry):
        src = behind(15 - s)
        pltpu.make_async_remote_copy(
            src_ref=outb.at[s], dst_ref=slots.at[src], send_sem=s2.at[s], recv_sem=r2.at[src],
            device_id=(g, ahead(15 - s) * 2 + c), device_id_type=MESH,
        ).wait_recv()
        pacc[...] += slots[src, 0:128, :].astype(F32)
        return carry

    lax.fori_loop(0, 15, arrive, 0)
    pre = pacc[...]
    weight = jnp.broadcast_to(w_out[...], (128, 128)).T
    gate = jax.nn.sigmoid(pre)
    logit = jnp.sum(pre * gate * weight, axis=0, keepdims=True)
    prob = jax.nn.sigmoid(logit)
    delta = gate * (1.0 + pre * (1.0 - gate)) * weight * (prob - labels[...])
    delta_low = delta.astype(BF)

    def norms(q, carry):
        acc, ssq = carry
        grad = split_dot(
            w_v[pl.ds(q * 8, 8)].reshape(1024, 128), delta_low, ((1,), (0,))
        )
        square = jnp.sum((grad * grad).reshape(8, 128, 128), axis=1)
        tail = slots[q, 128:144, :].astype(F32)
        return acc + square * tail[0:8], ssq + tail[8:16]

    acc, ssq = lax.fori_loop(
        0, 16, norms, (jnp.zeros((8, 128), F32), jnp.zeros((8, 128), F32))
    )
    norm_sq = jnp.sum(acc, axis=0, keepdims=True) + jnp.sum(
        ssq, axis=0, keepdims=True
    ) * jnp.sum(delta * delta, axis=0, keepdims=True)
    factor = CLIP / jnp.maximum(jnp.sqrt(norm_sq), CLIP)
    clip[t] = (factor * delta).T.astype(BF)

    def clip_copy(off):
        return pltpu.make_async_remote_copy(
            src_ref=clip.at[t], dst_ref=clip.at[t], send_sem=s3.at[off], recv_sem=r3.at[p],
            device_id=(g, ahead(off) * 2 + c), device_id_type=MESH,
        )

    def clip_arrival(off):
        src = behind(off)
        return pltpu.make_async_remote_copy(
            src_ref=clip.at[t], dst_ref=clip.at[src * 2 + c], send_sem=s3.at[off],
            recv_sem=r3.at[src], device_id=(g, ahead(off) * 2 + c), device_id_type=MESH,
        )

    def pass_on(off):
        src = behind(off)
        return pltpu.make_async_remote_copy(
            src_ref=clip.at[src * 2 + c], dst_ref=clip.at[src * 2 + c], send_sem=s4.at[off],
            recv_sem=r4.at[src], device_id=(g, sib), device_id_type=MESH,
        )

    def passed(off):
        src = behind(off)
        return pltpu.make_async_remote_copy(
            src_ref=clip.at[src * 2 + c], dst_ref=clip.at[src * 2 + 1 - c], send_sem=s4.at[off],
            recv_sem=r4.at[src], device_id=(g, sib), device_id_type=MESH,
        )

    def spread(off, carry):
        clip_copy(off).start()
        return carry

    pass_on(0).start()
    lax.fori_loop(1, 16, spread, 0)

    def pick_acc(n, carry):
        f = n // 64
        k = lax.rem(n, 64) * 8
        for i in range(8):
            value = accum_s[f, touched_s[f, k + i]]
            accb[f, pl.ds(k + i, 1), :] = jnp.full((1, 128), value, F32)
        return carry

    lax.fori_loop(0, 256, pick_acc, 0)

    for dy in range(4):
        for dx in range(4):
            off = dy * 4 + dx
            if off > 0:
                clip_arrival(off).wait_recv()
                pass_on(off).start()
        for dx in range(4):
            passed(dy * 4 + dx).wait_recv()
        row = lax.rem(y + 4 - dy, 4)
        b0 = pl.multiple_of(row * 1024, 1024)
        block = clip[pl.ds(row * 8, 8)].reshape(1024, 128)

        def add(i, carry):
            f = lax.rem(g + 1 + i, 4)
            part = split_dot(counts[f, :, pl.ds(b0, 1024)], block, ((1,), (0,)))
            if dy == 0:
                s_acc[f] = part
            elif dy < 3:
                s_acc[f] += part
            else:
                part = part + s_acc[f]
                s_acc[f] = part

                @pl.when(i < 3)
                def _():
                    zsend[i] = part.astype(BF)
                    pltpu.make_async_remote_copy(
                        src_ref=zsend.at[i], dst_ref=zrecv.at[g], send_sem=s5.at[i],
                        recv_sem=r5.at[g], device_id=(f, t), device_id_type=MESH,
                    ).start()

            return carry

        lax.fori_loop(0, 4, add, 0)

    summed = s_acc[g]
    for i in range(3):
        src = lax.rem(g + 3 - i, 4)
        pltpu.make_async_remote_copy(
            src_ref=zsend.at[i], dst_ref=zrecv.at[src], send_sem=s5.at[i], recv_sem=r5.at[src],
            device_id=(lax.rem(g + 1 + i, 4), t), device_id_type=MESH,
        ).wait_recv()
        summed = summed + zrecv[src].astype(F32)
    low = summed.astype(BF)
    rg[g] = split_dot(low, w_v[t * 4 + g], ((1,), (1,))).astype(BF)

    def row_copy(i):
        return pltpu.make_async_remote_copy(
            src_ref=rg.at[g], dst_ref=rg.at[g], send_sem=s6.at[i], recv_sem=r6.at[g],
            device_id=(lax.rem(g + 1 + i, 4), t), device_id_type=MESH,
        )

    def dense_copy(i):
        to = lax.rem(g + 1 + i, 4)
        return pltpu.make_async_remote_copy(
            src_ref=dsend.at[to], dst_ref=dense_out.at[g], send_sem=s7.at[i], recv_sem=r7.at[g],
            device_id=(to, t), device_id_type=MESH,
        )

    for i in range(3):
        row_copy(i).start()
    dsend[...] = split_dot(ttr[g], low, ((1,), (0,))).reshape(4, 32, 128)
    for i in range(3):
        dense_copy(i).start()
    dense_out[g] = dsend[g]

    diagonal = lax.broadcasted_iota(jnp.int32, (128, 128), 0) == lax.broadcasted_iota(
        jnp.int32, (128, 128), 1
    )

    def update(f):
        listed = rg[f].astype(F32) + noise[f]
        new_acc = accb[f] + jnp.sum(listed * listed, axis=1, keepdims=True) * (1.0 / 128.0)
        rows_out[f] = trows[f] - LEARN * listed / jnp.sqrt(new_acc)
        for q in range(4):
            tile = jnp.where(diagonal, new_acc[q * 128 : (q + 1) * 128, :], 0.0)
            nacc_out[f, q : q + 1, :] = jnp.sum(tile, axis=0, keepdims=True)

    update(g)
    for i in range(3):
        src = lax.rem(g + 3 - i, 4)
        pltpu.make_async_remote_copy(
            src_ref=rg.at[g], dst_ref=rg.at[src], send_sem=s6.at[i], recv_sem=r6.at[src],
            device_id=(lax.rem(g + 1 + i, 4), t), device_id_type=MESH,
        ).wait_recv()
        update(src)
    for i in range(3):
        src = lax.rem(g + 3 - i, 4)
        pltpu.make_async_remote_copy(
            src_ref=dsend.at[0], dst_ref=dense_out.at[src], send_sem=s7.at[i],
            recv_sem=r7.at[src], device_id=(lax.rem(g + 1 + i, 4), t), device_id_type=MESH,
        ).wait_recv()

    def drain(s, carry):
        sib_copy(s).wait_send()
        pass_on(s).wait_send()
        return carry

    def drain_far(s, carry):
        out_copy(s).wait_send()
        clip_copy(s + 1).wait_send()
        return carry

    lax.fori_loop(0, 16, drain, 0)
    lax.fori_loop(0, 15, drain_far, 0)
    for i in range(3):
        pltpu.make_async_remote_copy(
            src_ref=zsend.at[i], dst_ref=zrecv.at[g], send_sem=s5.at[i], recv_sem=r5.at[g],
            device_id=(lax.rem(g + 1 + i, 4), t), device_id_type=MESH,
        ).wait_send()
        row_copy(i).wait_send()
        dense_copy(i).wait_send()


def write_rows(touched_s, nacc_s, accum_h, table, rows, out, accum_out, acc_s, sem):
    f = pl.program_id(0)

    @pl.when(f == 0)
    def _():
        copy = pltpu.make_async_copy(accum_h, acc_s, sem)
        copy.start()
        copy.wait()

    out[...] = table[...]

    def put(n, carry):
        for i in range(8):
            k = n * 8 + i
            r = touched_s[f, k]
            out[0, pl.ds(r, 1), :] = rows[0, pl.ds(k, 1), :]
            acc_s[f, r] = nacc_s[f, k]
        return carry

    lax.fori_loop(0, 64, put, 0)

    @pl.when(f == 3)
    def _():
        copy = pltpu.make_async_copy(acc_s, accum_out, sem)
        copy.start()
        copy.wait()


def body(table, accum, w_hidden, w_out, ids, labels, touched, row_noise, dense_noise):
    vmem = pl.BlockSpec(memory_space=pltpu.VMEM)
    smem = pl.BlockSpec(memory_space=pltpu.SMEM)
    hbm = pl.BlockSpec(memory_space=pl.ANY)
    dma = pltpu.SemaphoreType.DMA
    rows, nacc, dense = pl.pallas_call(
        core,
        out_shape=(
            jax.ShapeDtypeStruct((4, 512, 128), F32),
            jax.ShapeDtypeStruct((4, 4, 128), F32),
            jax.ShapeDtypeStruct((4, 32, 128), F32),
        ),
        in_specs=[smem, smem, vmem, vmem, vmem, vmem, vmem, hbm, hbm],
        out_specs=(vmem, vmem, vmem),
        scratch_shapes=[
            pltpu.VMEM((4, 2048, 128), F32),
            pltpu.VMEM((128, 128, 128), BF),
            pltpu.VMEM((4, 512, 128), F32),
            pltpu.VMEM((4, 128, 512), BF),
            pltpu.VMEM((4, 512, 128), BF),
            pltpu.VMEM((128, 512), BF),
            pltpu.VMEM((4, 512, 4096), BF),
            pltpu.VMEM((512, 256), BF),
            pltpu.VMEM((16, 144, 128), F32),
            pltpu.VMEM((16, 144, 128), BF),
            pltpu.VMEM((16, 144, 128), BF),
            pltpu.VMEM((16, 144, 128), BF),
            pltpu.VMEM((16, 144, 128), BF),
            pltpu.VMEM((128, 128), F32),
            pltpu.VMEM((32, 128, 128), BF),
            pltpu.VMEM((4, 512, 128), F32),
            pltpu.VMEM((4, 512, 128), F32),
            pltpu.VMEM((3, 512, 128), BF),
            pltpu.VMEM((4, 512, 128), BF),
            pltpu.VMEM((4, 512, 128), BF),
            pltpu.VMEM((4, 32, 128), F32),
            dma((2,)),
            dma((16,)), dma((16,)), dma((16,)), dma((16,)),
            dma((16,)), dma((16,)), dma((16,)), dma((16,)),
            dma((3,)), dma((4,)), dma((3,)), dma((4,)), dma((3,)), dma((4,)),
        ],
        compiler_params=pltpu.CompilerParams(
            collective_id=0, has_side_effects=True, vmem_limit_bytes=56 * 1024 * 1024
        ),
        cost_estimate=pl.CostEstimate(
            flops=6 * 10**9, bytes_accessed=12 * 2**20, transcendentals=10**5
        ),
        name="step",
    )(
        touched, accum, ids, touched, w_out.reshape(1, 128), labels.reshape(1, 128),
        row_noise, table, w_hidden,
    )
    new_table, new_accum = pl.pallas_call(
        write_rows,
        grid=(4,),
        out_shape=(
            jax.ShapeDtypeStruct((4, 2048, 128), F32),
            jax.ShapeDtypeStruct((4, 2048), F32),
        ),
        in_specs=[
            smem, smem, hbm,
            pl.BlockSpec((1, 2048, 128), lambda f: (f, 0, 0)),
            pl.BlockSpec((1, 512, 128), lambda f: (f, 0, 0)),
        ],
        out_specs=(pl.BlockSpec((1, 2048, 128), lambda f: (f, 0, 0)), hbm),
        scratch_shapes=[pltpu.SMEM((4, 2048), F32), dma(())],
        compiler_params=pltpu.CompilerParams(vmem_limit_bytes=16 * 1024 * 1024),
        name="write_rows",
    )(touched, nacc.reshape(4, 512), accum, table, rows)
    return (new_table, new_accum, dense + dense_noise)


def solution(mesh):
    in_specs = (
        P("table", None, None),
        P("table", None),
        P(),
        P(),
        P("table", None, "group"),
        P(("group", "table")),
        P("table", None),
        P("table", None, None),
        P("table", "group", None),
    )
    out_specs = (P("table", None, None), P("table", None), P("table", "group", None))
    return jax.shard_map(body, mesh=mesh, in_specs=in_specs, out_specs=out_specs, check_vma=False)
```

time: 750 us -> 119 us (0.16)
  matrix products: 334 us -> 0 us
  blocking collectives: 183 us -> 0 us
  Pallas kernels: 0 us -> 114 us
  local copies, waits for them, and re-layouts: 109 us -> 1.94 us
  waiting for transfers between devices: 67.8 us -> 0 us
  other arithmetic: 28.4 us -> 1.48 us
  between operations: 15.8 us -> 0.69 us
    dot_general x19 -> x0, matrix products: 334 us -> none  [the longest x8 165 us: pool_block(): jnp.einsum('fbr,fre->bfe', counts, table_low, preferred_element_type=jnp....]
    psum x1 -> x0, blocking collectives: 124 us -> none  [body(): totals = lax.psum(embed_part + dense_part, 'table')]
    pallas_call x0 -> x2, Pallas kernels: none -> 114 us  [the longest x1 99.2 us: body(): pl.pallas_call(core, out_shape=(jax.ShapeDtypeStruct((4, 512, 128), F32),...]
    gather x4 -> x0, local copies, waits for them, and re-layouts: 61.7 us -> none  [pick_rows(): return source[where]]
    all_to_all x1 -> x0, blocking collectives: 58.2 us -> none  [body(): lax.all_to_all(pooled, 'table', split_axis=0, concat_axis=1, tiled=True)]
    all_to_all x1 -> x0, waiting for transfers between devices: 49.4 us -> none  [body(): lax.all_to_all(grad_pool, 'table', split_axis=1, concat_axis=0, tiled=True)]
    unnamed x28 -> x11, local copies, waits for them, and re-layouts: 22.8 us -> 1.94 us
    convert_element_type x5 -> x0, other arithmetic: 16.3 us -> none  [the longest x2 7.63 us: body(): summed = lax.psum(grads.astype(jnp.bfloat16), 'group').astype(jnp.float32)]
  transfers between devices with their start and end apart: 4 -> 0, of which waited for: 3 -> 0; matrix products, arithmetic and copies ran while one was open for 13% -> 0% of each run, Pallas kernels for 0% -> 0%
where the time goes in v1:
time: 119 us; the launch traced here: 118 us
  Pallas kernels  114 us (96%)
  local copies, waits for them, and re-layouts  1.94 us (2%)
  other arithmetic  1.48 us (1%)
    pallas_call x1, Pallas kernels, body(): pl.pallas_call(core, out_shape=(jax.ShapeDtypeStruct((4, 512, 128), F32),...  99.2 us
    pallas_call x1, Pallas kernels, body(): pl.pallas_call(write_rows, grid=(4,), out_shape=(jax.ShapeDtypeStruct((4,...  15.2 us

profile of v1, /device:TPU:0, one launch (start us, length us, event | category | flops | bytes accessed | tf_op | source)
XLA Modules:
  0.0 118.5 jit_solution(11249429206026517777)
XLA Ops:
  0.6 0.0 copy-start.4
  0.6 0.0 copy-start
  0.7 0.0 copy-start.2
  0.7 0.0 copy-start.3
  0.7 99.2 %step.1 = (f32[4,512,128]{2,1,0:T(8,128)}, f32[4,4,128]{2,1,0:T(4,128)}, f32[4,32,128]{2,1,0:T(8,128)}) custom-call(s32[4,512]{1,0:T(4,128)} %touched_s.3, f32[4,2048]{1,0:T(4,128)} %accum_h.1, s32[4,8,4096]{2,1,0:T(8,128)} %ids.1, s32[4,512]{1,0:T(4,128)} %touched_s.3, f32[1,128]{1,0:T(1,128)} %bitcast.8, f32[1,128]{1,0:T(1,128)} %bitcast.9, ...), custom_call_target="tpu_custom_call" | custom-call | flops 6000000000 | bytes 12582912 | tf_op jit(solution)/shard_map/step/pallas_call | solution.py:417
  99.8 0.7 copy.14
  100.5 0.0 copy-done.4
  100.5 1.5 %add.3 = f32[4,32,128]{2,1,0:T(8,128)} add(f32[4,32,128]{2,1,0:T(8,128)} %get-tuple-element.12, f32[4,32,128]{2,1,0:T(8,128)S(1)} %copy-done.4) | non-fusion elementwise | flops 16384 | bytes 196608 | tf_op jit(solution)/shard_map/add | solution.py:481
  102.0 0.0 copy-done
  102.0 0.0 copy-done.2
  102.0 0.0 copy-done.3
  102.0 0.0 copy-start.1
  102.0 1.2 %copy-done.1 = f32[4,512,128]{2,1,0:T(8,128)S(1)} copy-done((f32[4,512,128]{2,1,0:T(8,128)S(1)}, f32[4,512,128]{2,1,0:T(8,128)}, u32[]{:S(2)}) %copy-start.1) | copy-done | bytes 1048600
  103.3 15.2 %write_rows.1 = (f32[4,2048,128]{2,1,0:T(8,128)}, f32[4,2048]{1,0:T(4,128)}) custom-call(s32[4,512]{1,0:T(4,128)S(1)} %copy-done.3, f32[4,512]{1,0:T(4,128)S(1)} %bitcast.6, f32[4,2048]{1,0:T(4,128)S(1)} %copy-done.2, f32[4,2048,128]{2,1,0:T(8,128)S(1)} %copy-done, f32[4,512,128]{2,1,0:T(8,128)S(1)} %copy-done.1), custom_call_target="tpu_custom_call" | custom-call | tf_op jit(solution)/shard_map/write_rows/pallas_call | solution.py:464
Async XLA Ops:
  0.6 99.9 %copy-start.4 = (f32[4,32,128]{2,1,0:T(8,128)S(1)}, f32[4,32,128]{2,1,0:T(8,128)}, u32[]{:S(2)}) copy-start(f32[4,32,128]{2,1,0:T(8,128)} %param.17) | copy-start | bytes 196612
  0.6 101.4 %copy-start = (f32[4,2048,128]{2,1,0:T(8,128)S(1)}, f32[4,2048,128]{2,1,0:T(8,128)}, u32[]{:S(2)}) copy-start(f32[4,2048,128]{2,1,0:T(8,128)} %table.1) | copy-start | bytes 12582916
  0.7 101.4 %copy-start.2 = (f32[4,2048]{1,0:T(4,128)S(1)}, f32[4,2048]{1,0:T(4,128)}, u32[]{:S(2)}) copy-start(f32[4,2048]{1,0:T(4,128)} %accum_h.1) | copy-start | bytes 98308
  0.7 101.4 %copy-start.3 = (s32[4,512]{1,0:T(4,128)S(1)}, s32[4,512]{1,0:T(4,128)}, u32[]{:S(2)}) copy-start(s32[4,512]{1,0:T(4,128)} %touched_s.3) | copy-start | bytes 24580
  102.0 1.2 %copy-start.1 = (f32[4,512,128]{2,1,0:T(8,128)S(1)}, f32[4,512,128]{2,1,0:T(8,128)}, u32[]{:S(2)}) copy-start(f32[4,512,128]{2,1,0:T(8,128)} %get-tuple-element.9.rows) | copy-start | bytes 3145732

commit v2 on v1

--- a/solution.py
+++ b/solution.py
@@ -15,18 +15,14 @@
 LAG = 2
 
 
-def code_of(ids):
-    return lax.shift_left((ids & 127) + 128, lax.shift_right_logical(ids, 7)).astype(F32)
-
-
 def split_dot(a, b, dims):
     return lax.dot_general(a, b, (dims, ((), ())), preferred_element_type=F32)
 
 
 def core(
-    touched_s, accum_s, ids, touched_v, w_out, labels, noise, table_h, w_h,
-    rows_out, nacc_out, dense_out,
-    table_v, w_v, trows, ttr, tcode, wtr, counts, pool, keep, stage, sibin, outb, slots,
+    touched_s, accum, ids, touched_v, w_out, labels, noise, table_h, w_h,
+    rows_out, macc_out, dense_out,
+    table_v, w_v, trows, ttr, smap, low_col, wtr, counts, pool, keep, stage, sibin, outb, slots,
     pacc, clip, accb, s_acc, zsend, zrecv, rg, dsend,
     load_sem, s1, r1, s2, r2, s3, r3, s4, r4, s5, r5, s6, r6, s7, r7,
 ):
@@ -64,23 +60,38 @@
             barrier, inc=1, device_id=(lax.rem(g + i, 4), t), device_id_type=MESH
         )
 
-    for f in range(4):
-        row = code_of(touched_v[f : f + 1, :])
+    high_of = lax.broadcasted_iota(jnp.int32, (16, 512), 0)
+    low_of = lax.broadcasted_iota(jnp.int32, (128, 512), 0)
+    lane = lax.broadcasted_iota(jnp.int32, (1, 512), 1)
+    for f in range(4):
+        row = touched_v[f : f + 1, :]
+        row_low = row & 127
+        is_high = high_of == lax.shift_right_logical(row, 7)
+        is_low = jnp.where(low_of == row_low, 1.0, 0.0).astype(BF)
+        number = jnp.concatenate(
+            [
+                jnp.where(is_high, lax.shift_right_logical(lane, 4), 0),
+                jnp.where(is_high, lane & 15, 0),
+            ],
+            axis=0,
+        )
+        pair = split_dot(number.astype(F32).astype(BF), is_low, ((1,), (1,)))
+        smap[f] = (pair[:16] * 16.0 + pair[16:]).astype(jnp.int32)
         for q in range(4):
-            wide = jnp.broadcast_to(row[:, q * 128 : (q + 1) * 128], (128, 128))
-            tcode[f, q * 128 : (q + 1) * 128, :] = wide.T.astype(BF)
+            wide = jnp.broadcast_to(row_low[:, q * 128 : (q + 1) * 128], (128, 128))
+            low_col[f, q * 128 : (q + 1) * 128, :] = wide.T
 
     load_table.wait()
 
     def pick(n, carry):
-        f = n // 64
-        k = lax.rem(n, 64) * 8
-        for i in range(8):
+        f = n // 16
+        k = lax.rem(n, 16) * 32
+        for i in range(32):
             r = touched_s[f, k + i]
             trows[f, pl.ds(k + i, 1), :] = table_v[f, pl.ds(r, 1), :]
         return carry
 
-    lax.fori_loop(0, 256, pick, 0)
+    lax.fori_loop(0, 64, pick, 0)
     for f in range(4):
         ttr[f] = trows[f].T.astype(BF)
 
@@ -90,6 +101,7 @@
 
     pl.semaphore_wait(barrier, 19)
 
+    words = lax.broadcasted_iota(jnp.int32, (64, 128), 0)
     rows16 = lax.broadcasted_iota(jnp.int32, (16, 256), 0)
 
     def relay(s):
@@ -114,53 +126,43 @@
     def step(s, carry):
         b0 = pl.multiple_of(ahead(15 - s) * 256, 256)
 
-        def feature(f, carry):
-            extra, sumsq = carry
+        extra = jnp.zeros((16, 256), F32)
+        sumsq = jnp.zeros((1, 256), F32)
+        for f in range(4):
             bag = ids[f, :, pl.ds(b0, 256)]
-            code = code_of(bag)
             mult = jnp.ones((8, 256), F32)
             for d in range(1, 8):
                 mult = mult + jnp.where(bag == pltpu.roll(bag, d, 0), 1.0, 0.0)
             repeats = jnp.sum(mult, axis=0, keepdims=True)
             extra = jnp.where(rows16 == c * 4 + f, repeats, extra)
-            codes = []
-            mults = []
+            halves = []
             for half in range(2):
-                lanes = slice(half * 128, half * 128 + 128)
-                codes.append(
-                    [jnp.broadcast_to(code[h : h + 1, lanes], (16, 128)).astype(BF) for h in range(8)]
+                part = bag[:, half * 128 : half * 128 + 128]
+                high = lax.shift_right_logical(part, 7)
+                low = part & 127
+                slot = jnp.zeros((8, 128), jnp.int32)
+                for q in range(16):
+                    row = jnp.broadcast_to(smap[f, q : q + 1, :], (8, 128))
+                    slot = jnp.where(high == q, jnp.take_along_axis(row, low, axis=1), slot)
+                word = slot & 63
+                digit = lax.shift_left(
+                    jnp.ones((8, 128), jnp.int32), lax.shift_right_logical(slot, 6) * 4
                 )
-                mults.append(
-                    [jnp.broadcast_to(mult[h : h + 1, lanes], (16, 128)).astype(BF) for h in range(8)]
-                )
-            total = jnp.zeros((128, 256), F32)
-            zero = jnp.zeros((16, 128), BF)
-            for part in range(2):
+                packed = jnp.zeros((64, 128), jnp.int32)
+                for h in range(8):
+                    packed = packed + jnp.where(words == word[h : h + 1], digit[h : h + 1], 0)
                 tiles = []
-                for kt in range(16):
-                    k0 = part * 256 + kt * 16
-                    want = tcode[f, k0 : k0 + 16, :]
-                    both = []
-                    for half in range(2):
-                        count = zero
-                        for h in range(8):
-                            count = jnp.where(want == codes[half][h], mults[half][h], count)
-                        both.append(count)
-                    tiles.append(jnp.concatenate(both, axis=1))
-                block = jnp.concatenate(tiles, axis=0)
-                counts[f, part * 256 : part * 256 + 256, pl.ds(b0, 256)] = block
-                total = total + split_dot(
-                    ttr[f, :, part * 256 : part * 256 + 256], block, ((1,), (0,))
-                )
-            low = total.astype(BF)
-            pool[pl.ds(pl.multiple_of(f * 128, 128), 128), :] = low
-            wide = low.astype(F32)
+                for i in range(8):
+                    one = lax.shift_right_logical(packed, 4 * i) if i else packed
+                    tiles.append((one & 15).astype(F32).astype(BF))
+                halves.append(jnp.concatenate(tiles, axis=0))
+            block = jnp.concatenate(halves, axis=1)
+            counts[f, :, pl.ds(b0, 256)] = block
+            pooled = split_dot(ttr[f], block, ((1,), (0,))).astype(BF)
+            pool[f * 128 : f * 128 + 128, :] = pooled
+            wide = pooled.astype(F32)
             sumsq = sumsq + jnp.sum(wide * wide, axis=0, keepdims=True)
-            return extra, sumsq
-
-        extra, sumsq = lax.fori_loop(
-            0, 4, feature, (jnp.zeros((16, 256), F32), jnp.zeros((1, 256), F32))
-        )
+
         high = sumsq.astype(BF).astype(F32)
         extra = jnp.where(rows16 == 8 + 2 * c, high, extra)
         extra = jnp.where(rows16 == 9 + 2 * c, sumsq - high, extra)
@@ -205,17 +207,32 @@
     delta = gate * (1.0 + pre * (1.0 - gate)) * weight * (prob - labels[...])
     delta_low = delta.astype(BF)
 
+    nothing = jnp.zeros((128, 128), BF)
+    twice = jnp.concatenate(
+        [
+            jnp.concatenate([delta_low, nothing], axis=1),
+            jnp.concatenate([nothing, delta_low], axis=1),
+        ],
+        axis=0,
+    )
+
     def norms(q, carry):
         acc, ssq = carry
-        grad = split_dot(
-            w_v[pl.ds(q * 8, 8)].reshape(1024, 128), delta_low, ((1,), (0,))
-        )
-        square = jnp.sum((grad * grad).reshape(8, 128, 128), axis=1)
-        tail = slots[q, 128:144, :].astype(F32)
-        return acc + square * tail[0:8], ssq + tail[8:16]
+        weights = w_v[pl.ds(q * 32, 32)]
+        side = jnp.concatenate(
+            [weights[:16].reshape(2048, 128), weights[16:].reshape(2048, 128)], axis=1
+        )
+        grad = split_dot(side, twice, ((1,), (0,)))
+        square = jnp.sum((grad * grad).reshape(16, 128, 256), axis=1)
+        for i in range(4):
+            tail = slots[q * 4 + i, 128:144, :].astype(F32)
+            half = square[:, :128] if i < 2 else square[:, 128:]
+            acc = acc + half[(i % 2) * 8 : (i % 2) * 8 + 8] * tail[0:8]
+            ssq = ssq + tail[8:16]
+        return acc, ssq
 
     acc, ssq = lax.fori_loop(
-        0, 16, norms, (jnp.zeros((8, 128), F32), jnp.zeros((8, 128), F32))
+        0, 4, norms, (jnp.zeros((8, 128), F32), jnp.zeros((8, 128), F32))
     )
     norm_sq = jnp.sum(acc, axis=0, keepdims=True) + jnp.sum(
         ssq, axis=0, keepdims=True
@@ -223,6 +240,16 @@
     factor = CLIP / jnp.maximum(jnp.sqrt(norm_sq), CLIP)
     clip[t] = (factor * delta).T.astype(BF)
 
+    def high_one(f):
+        row = lax.shift_right_logical(touched_v[pl.ds(f, 1), :], 7)
+        return jnp.where(high_of == row, 1.0, 0.0).astype(BF)
+
+    def three(values):
+        first = values.astype(BF)
+        rest = values - first.astype(F32)
+        second = rest.astype(BF)
+        return first, second, (rest - second.astype(F32)).astype(BF)
+
     def clip_copy(off):
         return pltpu.make_async_remote_copy(
             src_ref=clip.at[t], dst_ref=clip.at[t], send_sem=s3.at[off], recv_sem=r3.at[p],
@@ -257,15 +284,20 @@
     pass_on(0).start()
     lax.fori_loop(1, 16, spread, 0)
 
-    def pick_acc(n, carry):
-        f = n // 64
-        k = lax.rem(n, 64) * 8
-        for i in range(8):
-            value = accum_s[f, touched_s[f, k + i]]
-            accb[f, pl.ds(k + i, 1), :] = jnp.full((1, 128), value, F32)
-        return carry
-
-    lax.fori_loop(0, 256, pick_acc, 0)
+    lanes = lax.broadcasted_iota(jnp.int32, (512, 128), 1)
+    for f in range(4):
+        is_high = high_one(f)
+        values = jnp.concatenate(
+            [accum[f : f + 1, q * 128 : (q + 1) * 128] for q in range(16)], axis=0
+        )
+        first, second, third = three(values)
+        spread_out = split_dot(
+            jnp.concatenate([is_high, is_high, is_high], axis=0),
+            jnp.concatenate([first, second, third], axis=0),
+            ((0,), (0,)),
+        )
+        found = jnp.where(lanes == low_col[f], spread_out, 0.0)
+        accb[f] = jnp.broadcast_to(jnp.sum(found, axis=1, keepdims=True), (512, 128))
 
     for dy in range(4):
         for dx in range(4):
@@ -333,17 +365,18 @@
         dense_copy(i).start()
     dense_out[g] = dsend[g]
 
-    diagonal = lax.broadcasted_iota(jnp.int32, (128, 128), 0) == lax.broadcasted_iota(
-        jnp.int32, (128, 128), 1
-    )
-
     def update(f):
         listed = rg[f].astype(F32) + noise[f]
-        new_acc = accb[f] + jnp.sum(listed * listed, axis=1, keepdims=True) * (1.0 / 128.0)
+        mean = jnp.sum(listed * listed, axis=1, keepdims=True) * (1.0 / 128.0)
+        new_acc = accb[f] + mean
         rows_out[f] = trows[f] - LEARN * listed / jnp.sqrt(new_acc)
-        for q in range(4):
-            tile = jnp.where(diagonal, new_acc[q * 128 : (q + 1) * 128, :], 0.0)
-            nacc_out[f, q : q + 1, :] = jnp.sum(tile, axis=0, keepdims=True)
+        is_high = high_one(f)
+        first, second, third = three(jnp.where(lanes == low_col[f], mean, 0.0))
+        macc_out[f] = (
+            split_dot(is_high, first, ((1,), (0,)))
+            + split_dot(is_high, second, ((1,), (0,)))
+            + split_dot(is_high, third, ((1,), (0,)))
+        )
 
     update(g)
     for i in range(3):
@@ -381,32 +414,36 @@
         dense_copy(i).wait_send()
 
 
-def write_rows(touched_s, nacc_s, accum_h, table, rows, out, accum_out, acc_s, sem):
-    f = pl.program_id(0)
-
-    @pl.when(f == 0)
-    def _():
-        copy = pltpu.make_async_copy(accum_h, acc_s, sem)
-        copy.start()
-        copy.wait()
-
-    out[...] = table[...]
-
-    def put(n, carry):
-        for i in range(8):
-            k = n * 8 + i
-            r = touched_s[f, k]
-            out[0, pl.ds(r, 1), :] = rows[0, pl.ds(k, 1), :]
-            acc_s[f, r] = nacc_s[f, k]
-        return carry
-
-    lax.fori_loop(0, 64, put, 0)
-
-    @pl.when(f == 3)
-    def _():
-        copy = pltpu.make_async_copy(acc_s, accum_out, sem)
-        copy.start()
-        copy.wait()
+def write_rows(
+    touched_s, accum, macc, dense, dense_noise, table_h, rows,
+    table_out, accum_out, dense_out, block, in_sem, out_sem,
+):
+    def load(f):
+        return pltpu.make_async_copy(table_h.at[f], block.at[f], in_sem.at[f])
+
+    def save(f):
+        return pltpu.make_async_copy(block.at[f], table_out.at[f], out_sem.at[f])
+
+    for f in range(4):
+        load(f).start()
+    dense_out[...] = dense[...] + dense_noise[...]
+    for f in range(4):
+        for q in range(16):
+            lanes = slice(q * 128, (q + 1) * 128)
+            accum_out[f : f + 1, lanes] = accum[f : f + 1, lanes] + macc[f, q : q + 1, :]
+    for f in range(4):
+        load(f).wait()
+
+        def put(n, carry):
+            k = pl.multiple_of(n * 32, 32)
+            for i in range(32):
+                block[f, pl.ds(touched_s[f, k + i], 1), :] = rows[f, pl.ds(k + i, 1), :]
+            return carry
+
+        lax.fori_loop(0, 16, put, 0)
+        save(f).start()
+    for f in range(4):
+        save(f).wait()
 
 
 def body(table, accum, w_hidden, w_out, ids, labels, touched, row_noise, dense_noise):
@@ -414,21 +451,22 @@
     smem = pl.BlockSpec(memory_space=pltpu.SMEM)
     hbm = pl.BlockSpec(memory_space=pl.ANY)
     dma = pltpu.SemaphoreType.DMA
-    rows, nacc, dense = pl.pallas_call(
+    rows, macc, dense = pl.pallas_call(
         core,
         out_shape=(
             jax.ShapeDtypeStruct((4, 512, 128), F32),
-            jax.ShapeDtypeStruct((4, 4, 128), F32),
+            jax.ShapeDtypeStruct((4, 16, 128), F32),
             jax.ShapeDtypeStruct((4, 32, 128), F32),
         ),
-        in_specs=[smem, smem, vmem, vmem, vmem, vmem, vmem, hbm, hbm],
+        in_specs=[smem, vmem, vmem, vmem, vmem, vmem, vmem, hbm, hbm],
         out_specs=(vmem, vmem, vmem),
         scratch_shapes=[
             pltpu.VMEM((4, 2048, 128), F32),
             pltpu.VMEM((128, 128, 128), BF),
             pltpu.VMEM((4, 512, 128), F32),
             pltpu.VMEM((4, 128, 512), BF),
-            pltpu.VMEM((4, 512, 128), BF),
+            pltpu.VMEM((4, 16, 128), jnp.int32),
+            pltpu.VMEM((4, 512, 128), jnp.int32),
             pltpu.VMEM((128, 512), BF),
             pltpu.VMEM((4, 512, 4096), BF),
             pltpu.VMEM((512, 256), BF),
@@ -461,24 +499,19 @@
         touched, accum, ids, touched, w_out.reshape(1, 128), labels.reshape(1, 128),
         row_noise, table, w_hidden,
     )
-    new_table, new_accum = pl.pallas_call(
+    return pl.pallas_call(
         write_rows,
-        grid=(4,),
         out_shape=(
             jax.ShapeDtypeStruct((4, 2048, 128), F32),
             jax.ShapeDtypeStruct((4, 2048), F32),
+            jax.ShapeDtypeStruct((4, 32, 128), F32),
         ),
-        in_specs=[
-            smem, smem, hbm,
-            pl.BlockSpec((1, 2048, 128), lambda f: (f, 0, 0)),
-            pl.BlockSpec((1, 512, 128), lambda f: (f, 0, 0)),
-        ],
-        out_specs=(pl.BlockSpec((1, 2048, 128), lambda f: (f, 0, 0)), hbm),
-        scratch_shapes=[pltpu.SMEM((4, 2048), F32), dma(())],
+        in_specs=[smem, vmem, vmem, vmem, vmem, hbm, vmem],
+        out_specs=(hbm, vmem, vmem),
+        scratch_shapes=[pltpu.VMEM((4, 2048, 128), F32), dma((4,)), dma((4,))],
         compiler_params=pltpu.CompilerParams(vmem_limit_bytes=16 * 1024 * 1024),
         name="write_rows",
-    )(touched, nacc.reshape(4, 512), accum, table, rows)
-    return (new_table, new_accum, dense + dense_noise)
+    )(touched, accum, macc, dense, dense_noise, table, rows)
 
 
 def solution(mesh):

time: 119 us -> 84.6 us (0.71)
  Pallas kernels: 114 us -> 80.7 us
  other arithmetic: 1.48 us -> 0 us
    pallas_call x1, Pallas kernels: 99.2 us -> 73.6 us  [body(): pl.pallas_call(core, out_shape=(jax.ShapeDtypeStruct((4, 512, 128), F32),...]
    pallas_call x1, Pallas kernels: 15.2 us -> 7.15 us  [body(): pl.pallas_call(write_rows, out_shape=(jax.ShapeDtypeStruct((4, 2048, 128)...]
    add x1 -> x0, other arithmetic: 1.48 us -> none  [body(): return (new_table, new_accum, dense + dense_noise)]
    unnamed x11 -> x14, local copies, waits for them, and re-layouts: 1.94 us -> 2.83 us
where the time goes in v2:
time: 84.6 us; the launch traced here: 84.3 us
  Pallas kernels  80.7 us (95%)
  local copies, waits for them, and re-layouts  2.83 us (3%)
    pallas_call x1, Pallas kernels, body(): pl.pallas_call(core, out_shape=(jax.ShapeDtypeStruct((4, 512, 128), F32),...  73.6 us
    pallas_call x1, Pallas kernels, body(): pl.pallas_call(write_rows, out_shape=(jax.ShapeDtypeStruct((4, 2048, 128)...  7.15 us
    unnamed x14, local copies, waits for them, and re-layouts  2.83 us

profile of v2, /device:TPU:0, one launch (start us, length us, event | category | flops | bytes accessed | tf_op | source)
XLA Modules:
  0.0 84.3 jit_solution(352521530435461424)
XLA Ops:
  0.6 0.0 copy-start
  0.6 0.0 copy-start.2
  0.7 0.0 copy-start.4
  0.7 0.0 copy-start.6
  0.7 73.6 %step.1 = (f32[4,512,128]{2,1,0:T(8,128)}, f32[4,16,128]{2,1,0:T(8,128)}, f32[4,32,128]{2,1,0:T(8,128)}) custom-call(s32[4,512]{1,0:T(4,128)} %touched_s.3, f32[4,2048]{1,0:T(4,128)} %accum.3, s32[4,8,4096]{2,1,0:T(8,128)} %ids.1, s32[4,512]{1,0:T(4,128)} %touched_s.3, f32[1,128]{1,0:T(1,128)} %bitcast.2, f32[1,128]{1,0:T(1,128)} %bitcast.3, ...), custom_call_target="tpu_custom_call" | custom-call | flops 6000000000 | bytes 12582912 | tf_op jit(solution)/shard_map/step/pallas_call | solution.py:454
  74.3 0.0 copy-done
  74.3 0.0 copy-done.2
  74.3 0.0 copy-done.4
  74.3 0.0 copy-done.6
  74.3 0.0 copy-start.1
  74.3 1.2 %copy-done.1 = f32[4,512,128]{2,1,0:T(8,128)S(1)} copy-done((f32[4,512,128]{2,1,0:T(8,128)S(1)}, f32[4,512,128]{2,1,0:T(8,128)}, u32[]{:S(2)}) %copy-start.1) | copy-done | bytes 1048600
  75.5 0.0 copy-start.3
  75.5 0.8 copy-done.3
  76.4 0.0 copy-start.5
  76.4 0.8 copy-done.5
  77.1 7.1 %write_rows.1 = (f32[4,2048,128]{2,1,0:T(8,128)}, f32[4,2048]{1,0:T(4,128)}, f32[4,32,128]{2,1,0:T(8,128)}) custom-call(s32[4,512]{1,0:T(4,128)S(1)} %copy-done.6, f32[4,2048]{1,0:T(4,128)S(1)} %copy-done.4, f32[4,16,128]{2,1,0:T(8,128)S(1)} %copy-done.5, f32[4,32,128]{2,1,0:T(8,128)S(1)} %copy-done.3, f32[4,32,128]{2,1,0:T(8,128)S(1)} %copy-done.2, ...), custom_call_target="tpu_custom_call" | custom-call | tf_op jit(solution)/shard_map/write_rows/pallas_call | solution.py:502
Async XLA Ops:
  0.6 73.6 %copy-start = (f32[4,2048,128]{2,1,0:T(8,128)S(1)}, f32[4,2048,128]{2,1,0:T(8,128)}, u32[]{:S(2)}) copy-start(f32[4,2048,128]{2,1,0:T(8,128)} %table_h.3) | copy-start | bytes 12582916
  0.6 73.6 %copy-start.2 = (f32[4,32,128]{2,1,0:T(8,128)S(1)}, f32[4,32,128]{2,1,0:T(8,128)}, u32[]{:S(2)}) copy-start(f32[4,32,128]{2,1,0:T(8,128)} %dense_noise.1) | copy-start | bytes 196612
  0.7 73.6 %copy-start.4 = (f32[4,2048]{1,0:T(4,128)S(1)}, f32[4,2048]{1,0:T(4,128)}, u32[]{:S(2)}) copy-start(f32[4,2048]{1,0:T(4,128)} %accum.3) | copy-start | bytes 98308
  0.7 73.6 %copy-start.6 = (s32[4,512]{1,0:T(4,128)S(1)}, s32[4,512]{1,0:T(4,128)}, u32[]{:S(2)}) copy-start(s32[4,512]{1,0:T(4,128)} %touched_s.3) | copy-start | bytes 24580
  74.3 1.2 %copy-start.1 = (f32[4,512,128]{2,1,0:T(8,128)S(1)}, f32[4,512,128]{2,1,0:T(8,128)}, u32[]{:S(2)}) copy-start(f32[4,512,128]{2,1,0:T(8,128)} %get-tuple-element.8.rows) | copy-start | bytes 3145732
  75.5 0.8 copy-start.3
  76.4 0.8 copy-start.5

commit v3 on v2

--- a/solution.py
+++ b/solution.py
@@ -12,7 +12,10 @@
 MESH = pl.DeviceIdType.MESH
 BF = jnp.bfloat16
 F32 = jnp.float32
-LAG = 2
+
+
+def scale_of(i):
+    return 16.0**i if i < 7 else 1.0
 
 
 def split_dot(a, b, dims):
@@ -22,9 +25,10 @@
 def core(
     touched_s, accum, ids, touched_v, w_out, labels, noise, table_h, w_h,
     rows_out, macc_out, dense_out,
-    table_v, w_v, trows, ttr, smap, low_col, wtr, counts, pool, keep, stage, sibin, outb, slots,
-    pacc, clip, accb, s_acc, zsend, zrecv, rg, dsend,
-    load_sem, s1, r1, s2, r2, s3, r3, s4, r4, s5, r5, s6, r6, s7, r7,
+    rows_v, macc_v, dense_v,
+    table_v, w_v, trows, ttr, smap, low_col, wtr, counts, ring, pool, bags, keep, stage, sibin,
+    outb, slots, pacc, clip, accb, s_acc, zsend, zrecv, rg, dsend,
+    load_sem, s1, r1, s2, r2, s3, r3, s4, r4, s5, r5, s6, r6, s7, r7, s8, r8, r9, out_sem,
 ):
     g = lax.axis_index("group")
     t = lax.axis_index("table")
@@ -40,9 +44,12 @@
     def behind(off):
         return lax.rem(y + 4 - off // 4, 4) * 4 + lax.rem(x + 4 - lax.rem(off, 4), 4)
 
-    load_table = pltpu.make_async_copy(table_h, table_v, load_sem.at[0])
-    load_w = pltpu.make_async_copy(w_h, w_v, load_sem.at[1])
-    load_table.start()
+    def load_table(f):
+        return pltpu.make_async_copy(table_h.at[f], table_v.at[f], load_sem.at[f])
+
+    for f in range(4):
+        load_table(f).start()
+    load_w = pltpu.make_async_copy(w_h, w_v, load_sem.at[4])
     load_w.start()
 
     barrier = pltpu.get_barrier_semaphore()
@@ -81,19 +88,61 @@
             wide = jnp.broadcast_to(row_low[:, q * 128 : (q + 1) * 128], (128, 128))
             low_col[f, q * 128 : (q + 1) * 128, :] = wide.T
 
-    load_table.wait()
-
-    def pick(n, carry):
-        f = n // 16
-        k = lax.rem(n, 16) * 32
-        for i in range(32):
-            r = touched_s[f, k + i]
-            trows[f, pl.ds(k + i, 1), :] = table_v[f, pl.ds(r, 1), :]
-        return carry
-
-    lax.fori_loop(0, 64, pick, 0)
-    for f in range(4):
-        ttr[f] = trows[f].T.astype(BF)
+    bags[...] = jnp.zeros((16, 8, 256), F32)
+    sublane = lax.broadcasted_iota(jnp.int32, (8, 128), 0)
+    scale = jnp.concatenate([jnp.full((64, 128), 1.0 / scale_of(i), F32) for i in range(8)], axis=0)
+
+    def count(s, f, target):
+        b0 = pl.multiple_of(ahead(15 - s) * 256, 256)
+        bag = ids[f, :, pl.ds(b0, 256)]
+        others = jnp.zeros((8, 256), F32)
+        for d in range(1, 5):
+            others = others + jnp.where(bag == pltpu.roll(bag, d, 0), 1.0 if d == 4 else 2.0, 0.0)
+        bags[s, pl.ds(f, 1), :] = 8.0 + jnp.sum(others, axis=0, keepdims=True)
+        halves = []
+        for half in range(2):
+            part = bag[:, half * 128 : half * 128 + 128]
+            high = lax.shift_right_logical(part, 7)
+            low = part & 127
+            slot = jnp.zeros((8, 128), jnp.int32)
+            for q in range(16):
+                row = jnp.broadcast_to(smap[f, q : q + 1, :], (8, 128))
+                slot = jnp.where(high == q, jnp.take_along_axis(row, low, axis=1), slot)
+            word = slot & 63
+            digit = lax.shift_left(
+                jnp.ones((8, 128), jnp.int32), lax.shift_right_logical(slot, 6) * 4
+            )
+            packed = [jnp.zeros((8, 128), jnp.int32) for _ in range(8)]
+            for h in range(8):
+                place = jnp.broadcast_to(word[h : h + 1], (8, 128)) - sublane
+                value = jnp.broadcast_to(digit[h : h + 1], (8, 128))
+                for v in range(8):
+                    packed[v] = packed[v] + jnp.where(place == 8 * v, value, 0)
+            packed = jnp.concatenate(packed, axis=0)
+            tiles = []
+            for i in range(7):
+                tiles.append((packed & (15 << (4 * i))).astype(F32).astype(BF))
+            tiles.append(lax.shift_right_logical(packed, 28).astype(F32).astype(BF))
+            halves.append(jnp.concatenate(tiles, axis=0))
+        block = jnp.concatenate(halves, axis=1)
+        target[f] = block
+        counts[f, :, pl.ds(b0, 256)] = block
+
+    def early(n, carry):
+        s = n // 4
+        f = lax.rem(n, 4)
+        count(s, f, ring.at[s])
+        k = f * 128
+        for i in range(128):
+            r = touched_s[s, k + i]
+            trows[s, pl.ds(k + i, 1), :] = table_v[s, pl.ds(r, 1), :]
+        return carry
+
+    for f in range(4):
+        load_table(f).wait()
+    lax.fori_loop(0, 16, early, 0)
+    for f in range(4):
+        ttr[f] = (trows[f] * scale).T.astype(BF)
 
     load_w.wait()
     for f in range(4):
@@ -101,8 +150,7 @@
 
     pl.semaphore_wait(barrier, 19)
 
-    words = lax.broadcasted_iota(jnp.int32, (64, 128), 0)
-    rows16 = lax.broadcasted_iota(jnp.int32, (16, 256), 0)
+    rows8 = lax.broadcasted_iota(jnp.int32, (8, 256), 0)
 
     def relay(s):
         pltpu.make_async_remote_copy(
@@ -123,67 +171,57 @@
             device_id=(g, sib), device_id_type=MESH,
         )
 
-    def step(s, carry):
-        b0 = pl.multiple_of(ahead(15 - s) * 256, 256)
-
-        extra = jnp.zeros((16, 256), F32)
+    def finish(s, source):
         sumsq = jnp.zeros((1, 256), F32)
         for f in range(4):
-            bag = ids[f, :, pl.ds(b0, 256)]
-            mult = jnp.ones((8, 256), F32)
-            for d in range(1, 8):
-                mult = mult + jnp.where(bag == pltpu.roll(bag, d, 0), 1.0, 0.0)
-            repeats = jnp.sum(mult, axis=0, keepdims=True)
-            extra = jnp.where(rows16 == c * 4 + f, repeats, extra)
-            halves = []
-            for half in range(2):
-                part = bag[:, half * 128 : half * 128 + 128]
-                high = lax.shift_right_logical(part, 7)
-                low = part & 127
-                slot = jnp.zeros((8, 128), jnp.int32)
-                for q in range(16):
-                    row = jnp.broadcast_to(smap[f, q : q + 1, :], (8, 128))
-                    slot = jnp.where(high == q, jnp.take_along_axis(row, low, axis=1), slot)
-                word = slot & 63
-                digit = lax.shift_left(
-                    jnp.ones((8, 128), jnp.int32), lax.shift_right_logical(slot, 6) * 4
-                )
-                packed = jnp.zeros((64, 128), jnp.int32)
-                for h in range(8):
-                    packed = packed + jnp.where(words == word[h : h + 1], digit[h : h + 1], 0)
-                tiles = []
-                for i in range(8):
-                    one = lax.shift_right_logical(packed, 4 * i) if i else packed
-                    tiles.append((one & 15).astype(F32).astype(BF))
-                halves.append(jnp.concatenate(tiles, axis=0))
-            block = jnp.concatenate(halves, axis=1)
-            counts[f, :, pl.ds(b0, 256)] = block
-            pooled = split_dot(ttr[f], block, ((1,), (0,))).astype(BF)
+            pooled = split_dot(ttr[f], source[f], ((1,), (0,))).astype(BF)
             pool[f * 128 : f * 128 + 128, :] = pooled
             wide = pooled.astype(F32)
             sumsq = sumsq + jnp.sum(wide * wide, axis=0, keepdims=True)
-
         high = sumsq.astype(BF).astype(F32)
-        extra = jnp.where(rows16 == 8 + 2 * c, high, extra)
-        extra = jnp.where(rows16 == 9 + 2 * c, sumsq - high, extra)
+        first = c == 0
+        repeats = bags[s]
+        repeats = jnp.where(first, repeats, pltpu.roll(repeats, 4, 0))
+        squares = jnp.where(rows8 == 2 * c, high, 0.0)
+        squares = jnp.where(rows8 == 2 * c + 1, sumsq - high, squares)
+        extra = jnp.concatenate([repeats, squares], axis=0)
         part = split_dot(wtr[...], pool[...], ((1,), (0,)))
-        first = c == 0
         keep[s, 0:128, :] = jnp.where(first, part[:, :128], part[:, 128:])
         keep[s, 128:144, :] = jnp.where(first, extra[:, :128], extra[:, 128:])
         stage[s, 0:128, :] = jnp.where(first, part[:, 128:], part[:, :128]).astype(BF)
         stage[s, 128:144, :] = jnp.where(first, extra[:, 128:], extra[:, :128]).astype(BF)
+
+    def send(s):
+        relay(s)
+        out_copy(s).start()
+
+    def catch_up(s, carry):
+        finish(s, ring.at[s])
         sib_copy(s).start()
-
-        @pl.when(s >= LAG)
-        def _():
-            relay(s - LAG)
-            out_copy(s - LAG).start()
-
-        return carry
-
-    lax.fori_loop(0, 16, step, 0)
-    relay(14)
-    out_copy(14).start()
+        return carry
+
+    lax.fori_loop(0, 3, catch_up, 0)
+    send(0)
+
+    def step(i, carry):
+        s = 4 + 2 * i
+        finish(s - 1, ring.at[3])
+        for f in range(4):
+            count(s, f, ring.at[0])
+        sib_copy(s - 1).start()
+        send(s - 3)
+        finish(s, ring.at[0])
+        for f in range(4):
+            count(s + 1, f, ring.at[3])
+        sib_copy(s).start()
+        send(s - 2)
+        return carry
+
+    lax.fori_loop(0, 6, step, 0)
+    finish(15, ring.at[3])
+    sib_copy(15).start()
+    send(13)
+    send(14)
     relay(15)
     slots[p] = outb[15]
 
@@ -250,39 +288,55 @@
         second = rest.astype(BF)
         return first, second, (rest - second.astype(F32)).astype(BF)
 
-    def clip_copy(off):
-        return pltpu.make_async_remote_copy(
-            src_ref=clip.at[t], dst_ref=clip.at[t], send_sem=s3.at[off], recv_sem=r3.at[p],
-            device_id=(g, ahead(off) * 2 + c), device_id_type=MESH,
-        )
-
-    def clip_arrival(off):
-        src = behind(off)
-        return pltpu.make_async_remote_copy(
-            src_ref=clip.at[t], dst_ref=clip.at[src * 2 + c], send_sem=s3.at[off],
-            recv_sem=r3.at[src], device_id=(g, ahead(off) * 2 + c), device_id_type=MESH,
-        )
-
-    def pass_on(off):
-        src = behind(off)
-        return pltpu.make_async_remote_copy(
-            src_ref=clip.at[src * 2 + c], dst_ref=clip.at[src * 2 + c], send_sem=s4.at[off],
+    def chip(down, over):
+        return lax.rem(y + 4 - down, 4) * 4 + lax.rem(x + 4 - over, 4)
+
+    def beside(i):
+        if i < 3:
+            return y * 4 + lax.rem(x + 1 + i, 4)
+        return lax.rem(y + i - 2, 4) * 4 + x
+
+    def clip_copy(i, src):
+        return pltpu.make_async_remote_copy(
+            src_ref=clip.at[src * 2 + c], dst_ref=clip.at[src * 2 + c], send_sem=s3.at[i],
+            recv_sem=r3.at[src], device_id=(g, beside(i) * 2 + c), device_id_type=MESH,
+        )
+
+    def half_copy(n, src):
+        upper = n % 6 < 3
+        rows = pl.ds(0, 64) if upper else pl.ds(64, 64)
+        return pltpu.make_async_remote_copy(
+            src_ref=clip.at[src * 2 + c, rows], dst_ref=clip.at[src * 2 + c, rows],
+            send_sem=s8.at[n], recv_sem=(r8 if upper else r9).at[src],
+            device_id=(g, beside(n % 3 + (3 if upper else 0)) * 2 + c), device_id_type=MESH,
+        )
+
+    def pass_on(src):
+        return pltpu.make_async_remote_copy(
+            src_ref=clip.at[src * 2 + c], dst_ref=clip.at[src * 2 + c], send_sem=s4.at[src],
             recv_sem=r4.at[src], device_id=(g, sib), device_id_type=MESH,
         )
 
-    def passed(off):
-        src = behind(off)
-        return pltpu.make_async_remote_copy(
-            src_ref=clip.at[src * 2 + c], dst_ref=clip.at[src * 2 + 1 - c], send_sem=s4.at[off],
+    def passed(src):
+        return pltpu.make_async_remote_copy(
+            src_ref=clip.at[src * 2 + c], dst_ref=clip.at[src * 2 + 1 - c], send_sem=s4.at[src],
             recv_sem=r4.at[src], device_id=(g, sib), device_id_type=MESH,
         )
 
-    def spread(off, carry):
-        clip_copy(off).start()
-        return carry
-
-    pass_on(0).start()
-    lax.fori_loop(1, 16, spread, 0)
+    for i in (0, 3, 2, 5, 1, 4):
+        clip_copy(i, p).start()
+    pass_on(p).start()
+    for i in (0, 2, 1):
+        src = chip(0, i + 1)
+        clip_copy(i, src).wait_recv()
+        for j in (0, 2, 1):
+            half_copy(i * 6 + j, src).start()
+        pass_on(src).start()
+        src = chip(i + 1, 0)
+        clip_copy(i, src).wait_recv()
+        for j in (3, 5, 4):
+            half_copy(i * 6 + j, src).start()
+        pass_on(src).start()
 
     lanes = lax.broadcasted_iota(jnp.int32, (512, 128), 1)
     for f in range(4):
@@ -299,41 +353,63 @@
         found = jnp.where(lanes == low_col[f], spread_out, 0.0)
         accb[f] = jnp.broadcast_to(jnp.sum(found, axis=1, keepdims=True), (512, 128))
 
-    for dy in range(4):
-        for dx in range(4):
-            off = dy * 4 + dx
-            if off > 0:
-                clip_arrival(off).wait_recv()
-                pass_on(off).start()
-        for dx in range(4):
-            passed(dy * 4 + dx).wait_recv()
-        row = lax.rem(y + 4 - dy, 4)
-        b0 = pl.multiple_of(row * 1024, 1024)
-        block = clip[pl.ds(row * 8, 8)].reshape(1024, 128)
-
-        def add(i, carry):
-            f = lax.rem(g + 1 + i, 4)
-            part = split_dot(counts[f, :, pl.ds(b0, 1024)], block, ((1,), (0,)))
-            if dy == 0:
-                s_acc[f] = part
-            elif dy < 3:
-                s_acc[f] += part
-            else:
-                part = part + s_acc[f]
-                s_acc[f] = part
-
-                @pl.when(i < 3)
-                def _():
-                    zsend[i] = part.astype(BF)
-                    pltpu.make_async_remote_copy(
-                        src_ref=zsend.at[i], dst_ref=zrecv.at[g], send_sem=s5.at[i],
-                        recv_sem=r5.at[g], device_id=(f, t), device_id_type=MESH,
-                    ).start()
-
-            return carry
-
-        lax.fori_loop(0, 4, add, 0)
-
+    def diagonals(down):
+        for over in (1, 3, 2):
+            src = chip(down, over)
+            half_copy(0, src).wait_recv()
+            half_copy(3, src).wait_recv()
+            pass_on(src).start()
+
+    def product(f, src, chips):
+        b0 = pl.multiple_of(src * 256, 256)
+        block = clip[pl.ds(src * 2, 2 * chips)].reshape(256 * chips, 128)
+        return split_dot(counts[f, :, pl.ds(b0, 256 * chips)], block, ((1,), (0,)))
+
+    for over in range(4):
+        passed(chip(0, over)).wait_recv()
+
+    def own_row(f, carry):
+        s_acc[f] = product(f, y * 4, 4)
+        return carry
+
+    lax.fori_loop(0, 4, own_row, 0)
+    diagonals(1)
+    for down in (1, 3, 2):
+        passed(chip(down, 0)).wait_recv()
+    diagonals(3)
+
+    def own_column(f, carry):
+        s_acc[f] += (
+            product(f, chip(1, 0), 1) + product(f, chip(3, 0), 1) + product(f, chip(2, 0), 1)
+        )
+        return carry
+
+    lax.fori_loop(0, 4, own_column, 0)
+    diagonals(2)
+    for down in (1, 3, 2):
+        for over in (1, 3, 2):
+            passed(chip(down, over)).wait_recv()
+
+    def other_blocks(i, carry):
+        f = lax.rem(g + 1 + i, 4)
+        part = s_acc[f]
+        for down in (1, 3, 2):
+            for over in (1, 3, 2):
+                part = part + product(f, chip(down, over), 1)
+        part = part * scale
+        s_acc[f] = part
+
+        @pl.when(i < 3)
+        def _():
+            zsend[i] = part.astype(BF)
+            pltpu.make_async_remote_copy(
+                src_ref=zsend.at[i], dst_ref=zrecv.at[g], send_sem=s5.at[i],
+                recv_sem=r5.at[g], device_id=(f, t), device_id_type=MESH,
+            ).start()
+
+        return carry
+
+    lax.fori_loop(0, 4, other_blocks, 0)
     summed = s_acc[g]
     for i in range(3):
         src = lax.rem(g + 3 - i, 4)
@@ -354,29 +430,33 @@
     def dense_copy(i):
         to = lax.rem(g + 1 + i, 4)
         return pltpu.make_async_remote_copy(
-            src_ref=dsend.at[to], dst_ref=dense_out.at[g], send_sem=s7.at[i], recv_sem=r7.at[g],
+            src_ref=dsend.at[to], dst_ref=dense_v.at[g], send_sem=s7.at[i], recv_sem=r7.at[g],
             device_id=(to, t), device_id_type=MESH,
         )
 
     for i in range(3):
         row_copy(i).start()
-    dsend[...] = split_dot(ttr[g], low, ((1,), (0,))).reshape(4, 32, 128)
+    dsend[...] = split_dot(trows[g].T.astype(BF), low, ((1,), (0,))).reshape(4, 32, 128)
     for i in range(3):
         dense_copy(i).start()
-    dense_out[g] = dsend[g]
+    dense_v[g] = dsend[g]
+
+    def rows_save(f):
+        return pltpu.make_async_copy(rows_v.at[f], rows_out.at[f], out_sem.at[f])
 
     def update(f):
         listed = rg[f].astype(F32) + noise[f]
         mean = jnp.sum(listed * listed, axis=1, keepdims=True) * (1.0 / 128.0)
         new_acc = accb[f] + mean
-        rows_out[f] = trows[f] - LEARN * listed / jnp.sqrt(new_acc)
+        rows_v[f] = trows[f] - LEARN * listed / jnp.sqrt(new_acc)
         is_high = high_one(f)
         first, second, third = three(jnp.where(lanes == low_col[f], mean, 0.0))
-        macc_out[f] = (
+        macc_v[f] = (
             split_dot(is_high, first, ((1,), (0,)))
             + split_dot(is_high, second, ((1,), (0,)))
             + split_dot(is_high, third, ((1,), (0,)))
         )
+        rows_save(f).start()
 
     update(g)
     for i in range(3):
@@ -389,9 +469,16 @@
     for i in range(3):
         src = lax.rem(g + 3 - i, 4)
         pltpu.make_async_remote_copy(
-            src_ref=dsend.at[0], dst_ref=dense_out.at[src], send_sem=s7.at[i],
+            src_ref=dsend.at[0], dst_ref=dense_v.at[src], send_sem=s7.at[i],
             recv_sem=r7.at[src], device_id=(lax.rem(g + 1 + i, 4), t), device_id_type=MESH,
         ).wait_recv()
+
+    saves = [
+        pltpu.make_async_copy(macc_v, macc_out, out_sem.at[4]),
+        pltpu.make_async_copy(dense_v, dense_out, out_sem.at[5]),
+    ]
+    for save in saves:
+        save.start()
 
     def drain(s, carry):
         sib_copy(s).wait_send()
@@ -400,11 +487,14 @@
 
     def drain_far(s, carry):
         out_copy(s).wait_send()
-        clip_copy(s + 1).wait_send()
         return carry
 
     lax.fori_loop(0, 16, drain, 0)
     lax.fori_loop(0, 15, drain_far, 0)
+    for i in range(6):
+        clip_copy(i, p).wait_send()
+    for n in range(18):
+        half_copy(n, p).wait_send()
     for i in range(3):
         pltpu.make_async_remote_copy(
             src_ref=zsend.at[i], dst_ref=zrecv.at[g], send_sem=s5.at[i], recv_sem=r5.at[g],
@@ -412,36 +502,67 @@
         ).wait_send()
         row_copy(i).wait_send()
         dense_copy(i).wait_send()
+    for f in range(4):
+        rows_save(f).wait()
+    for save in saves:
+        save.wait()
 
 
 def write_rows(
-    touched_s, accum, macc, dense, dense_noise, table_h, rows,
-    table_out, accum_out, dense_out, block, in_sem, out_sem,
+    touched_h, accum_h, macc_h, dense_h, noise_h, table_h, rows_h,
+    table_out, accum_out, dense_out,
+    touched_s, accum, macc, dense, noise, block, rows, sem, in_sem, rows_sem, out_sem,
 ):
     def load(f):
         return pltpu.make_async_copy(table_h.at[f], block.at[f], in_sem.at[f])
 
+    def load_rows(f):
+        return pltpu.make_async_copy(rows_h.at[f], rows.at[f], rows_sem.at[f])
+
     def save(f):
         return pltpu.make_async_copy(block.at[f], table_out.at[f], out_sem.at[f])
 
-    for f in range(4):
+    load(0).start()
+    load_rows(0).start()
+    small = [
+        pltpu.make_async_copy(source, target, sem.at[i])
+        for i, (source, target) in enumerate(
+            (
+                (touched_h, touched_s), (accum_h, accum), (macc_h, macc),
+                (dense_h, dense), (noise_h, noise),
+            )
+        )
+    ]
+    for copy in small:
+        copy.start()
+    for f in range(1, 4):
         load(f).start()
-    dense_out[...] = dense[...] + dense_noise[...]
+        load_rows(f).start()
+    for copy in small:
+        copy.wait()
+    dense[...] += noise[...]
+    save_dense = pltpu.make_async_copy(dense, dense_out, sem.at[5])
+    save_dense.start()
     for f in range(4):
         for q in range(16):
             lanes = slice(q * 128, (q + 1) * 128)
-            accum_out[f : f + 1, lanes] = accum[f : f + 1, lanes] + macc[f, q : q + 1, :]
+            accum[f : f + 1, lanes] += macc[f, q : q + 1, :]
+    save_accum = pltpu.make_async_copy(accum, accum_out, sem.at[6])
+    save_accum.start()
     for f in range(4):
         load(f).wait()
+        load_rows(f).wait()
 
         def put(n, carry):
-            k = pl.multiple_of(n * 32, 32)
-            for i in range(32):
+            k = pl.multiple_of(n * 64, 64)
+            for i in range(64):
                 block[f, pl.ds(touched_s[f, k + i], 1), :] = rows[f, pl.ds(k + i, 1), :]
             return carry
 
-        lax.fori_loop(0, 16, put, 0)
+        lax.fori_loop(0, 8, put, 0)
         save(f).start()
+    save_dense.wait()
+    save_accum.wait()
     for f in range(4):
         save(f).wait()
 
@@ -450,6 +571,7 @@
     vmem = pl.BlockSpec(memory_space=pltpu.VMEM)
     smem = pl.BlockSpec(memory_space=pltpu.SMEM)
     hbm = pl.BlockSpec(memory_space=pl.ANY)
+    far = pl.BlockSpec(memory_space=pltpu.HBM)
     dma = pltpu.SemaphoreType.DMA
     rows, macc, dense = pl.pallas_call(
         core,
@@ -459,8 +581,11 @@
             jax.ShapeDtypeStruct((4, 32, 128), F32),
         ),
         in_specs=[smem, vmem, vmem, vmem, vmem, vmem, vmem, hbm, hbm],
-        out_specs=(vmem, vmem, vmem),
+        out_specs=(far, far, far),
         scratch_shapes=[
+            pltpu.VMEM((4, 512, 128), F32),
+            pltpu.VMEM((4, 16, 128), F32),
+            pltpu.VMEM((4, 32, 128), F32),
             pltpu.VMEM((4, 2048, 128), F32),
             pltpu.VMEM((128, 128, 128), BF),
             pltpu.VMEM((4, 512, 128), F32),
@@ -469,7 +594,9 @@
             pltpu.VMEM((4, 512, 128), jnp.int32),
             pltpu.VMEM((128, 512), BF),
             pltpu.VMEM((4, 512, 4096), BF),
+            pltpu.VMEM((4, 4, 512, 256), BF),
             pltpu.VMEM((512, 256), BF),
+            pltpu.VMEM((16, 8, 256), F32),
             pltpu.VMEM((16, 144, 128), F32),
             pltpu.VMEM((16, 144, 128), BF),
             pltpu.VMEM((16, 144, 128), BF),
@@ -483,10 +610,11 @@
             pltpu.VMEM((4, 512, 128), BF),
             pltpu.VMEM((4, 512, 128), BF),
             pltpu.VMEM((4, 32, 128), F32),
-            dma((2,)),
+            dma((5,)),
             dma((16,)), dma((16,)), dma((16,)), dma((16,)),
-            dma((16,)), dma((16,)), dma((16,)), dma((16,)),
+            dma((6,)), dma((16,)), dma((16,)), dma((16,)),
             dma((3,)), dma((4,)), dma((3,)), dma((4,)), dma((3,)), dma((4,)),
+            dma((18,)), dma((16,)), dma((16,)), dma((6,)),
         ],
         compiler_params=pltpu.CompilerParams(
             collective_id=0, has_side_effects=True, vmem_limit_bytes=56 * 1024 * 1024
@@ -506,10 +634,19 @@
             jax.ShapeDtypeStruct((4, 2048), F32),
             jax.ShapeDtypeStruct((4, 32, 128), F32),
         ),
-        in_specs=[smem, vmem, vmem, vmem, vmem, hbm, vmem],
-        out_specs=(hbm, vmem, vmem),
-        scratch_shapes=[pltpu.VMEM((4, 2048, 128), F32), dma((4,)), dma((4,))],
-        compiler_params=pltpu.CompilerParams(vmem_limit_bytes=16 * 1024 * 1024),
+        in_specs=[hbm] * 7,
+        out_specs=(hbm, hbm, hbm),
+        scratch_shapes=[
+            pltpu.SMEM((4, 512), jnp.int32),
+            pltpu.VMEM((4, 2048), F32),
+            pltpu.VMEM((4, 16, 128), F32),
+            pltpu.VMEM((4, 32, 128), F32),
+            pltpu.VMEM((4, 32, 128), F32),
+            pltpu.VMEM((4, 2048, 128), F32),
+            pltpu.VMEM((4, 512, 128), F32),
+            dma((7,)), dma((4,)), dma((4,)), dma((4,)),
+        ],
+        compiler_params=pltpu.CompilerParams(vmem_limit_bytes=60 * 1024 * 1024),
         name="write_rows",
     )(touched, accum, macc, dense, dense_noise, table, rows)
 

time: 84.6 us -> 77.4 us (0.915)
  Pallas kernels: 80.7 us -> 76.7 us
  local copies, waits for them, and re-layouts: 2.83 us -> 0 us
    pallas_call x1, Pallas kernels: 73.6 us -> 69.1 us  [body(): pl.pallas_call(core, out_shape=(jax.ShapeDtypeStruct((4, 512, 128), F32),...]
    unnamed x14 -> x0, local copies, waits for them, and re-layouts: 2.83 us -> none
where the time goes in v3:
time: 77.4 us; the launch traced here: 77.3 us
  Pallas kernels  76.7 us (99%)
    pallas_call x1, Pallas kernels, body(): pl.pallas_call(core, out_shape=(jax.ShapeDtypeStruct((4, 512, 128), F32),...  69.1 us
    pallas_call x1, Pallas kernels, body(): pl.pallas_call(write_rows, out_shape=(jax.ShapeDtypeStruct((4, 2048, 128)...  7.59 us

profile of v3, /device:TPU:0, one launch (start us, length us, event | category | flops | bytes accessed | tf_op | source)
XLA Modules:
  0.0 77.3 jit_solution(7044206972835023887)
XLA Ops:
  0.6 69.1 %step.1 = (f32[4,512,128]{2,1,0:T(8,128)}, f32[4,16,128]{2,1,0:T(8,128)}, f32[4,32,128]{2,1,0:T(8,128)}) custom-call(s32[4,512]{1,0:T(4,128)} %touched_h.1, f32[4,2048]{1,0:T(4,128)} %accum_h.1, s32[4,8,4096]{2,1,0:T(8,128)} %ids.1, s32[4,512]{1,0:T(4,128)} %touched_h.1, f32[1,128]{1,0:T(1,128)} %bitcast.2, f32[1,128]{1,0:T(1,128)} %bitcast.3, ...), custom_call_target="tpu_custom_call" | custom-call | flops 6000000000 | bytes 12582912 | tf_op jit(solution)/shard_map/step/pallas_call | solution.py:576
  69.7 7.6 %write_rows.1 = (f32[4,2048,128]{2,1,0:T(8,128)}, f32[4,2048]{1,0:T(4,128)}, f32[4,32,128]{2,1,0:T(8,128)}) custom-call(s32[4,512]{1,0:T(4,128)} %touched_h.1, f32[4,2048]{1,0:T(4,128)} %accum_h.1, f32[4,16,128]{2,1,0:T(8,128)} %get-tuple-element.6.macc_h, f32[4,32,128]{2,1,0:T(8,128)} %get-tuple-element.7.dense_h, f32[4,32,128]{2,1,0:T(8,128)} %noise_h.1, ...), custom_call_target="tpu_custom_call" | custom-call | tf_op jit(solution)/shard_map/write_rows/pallas_call | solution.py:630

commit v4 on v3

v4 whole, which is shorter than its diff:
```python
import functools

import jax
import jax.numpy as jnp
from jax import lax
from jax.experimental import pallas as pl
from jax.experimental.pallas import tpu as pltpu
from jax.sharding import PartitionSpec as P

CLIP = 1.0
LEARN = 0.05
MESH = pl.DeviceIdType.MESH
BF = jnp.bfloat16
F32 = jnp.float32


def scale_of(i):
    return 16.0**i if i < 7 else 1.0


def split_dot(a, b, dims):
    return lax.dot_general(a, b, (dims, ((), ())), preferred_element_type=F32)


def core(
    touched_h, accum_h, ids_h, w_out_h, labels_h, noise_h, table_h, w_h,
    rows_out, macc_out, dense_out,
    touched_s, touched_v, accum, ids, w_out, labels, noise, rows_v, macc_v, dense_v,
    table_v, w_v, trows, ttr, smap, low_col, counts, ring, bags, both_ids, send_ids,
    outb, slots, pacc, clip, accb, s_acc, half_send, half_recv, zsend, zrecv, rg, dsend,
    load_sem, s1, r1, s2, r2, s3, r3, s4, r4, s5, r5, s6, r6, s7, r7, out_sem,
):
    g = lax.axis_index("group")
    t = lax.axis_index("table")
    c = lax.rem(t, 2)
    p = t // 2
    y = p // 4
    x = lax.rem(p, 4)
    sib = t + 1 - 2 * c

    def ahead(off):
        return lax.rem(y + off // 4, 4) * 4 + lax.rem(x + lax.rem(off, 4), 4)

    def behind(off):
        return lax.rem(y + 4 - off // 4, 4) * 4 + lax.rem(x + 4 - lax.rem(off, 4), 4)

    loads = [
        pltpu.make_async_copy(source, target, load_sem.at[i])
        for i, (source, target) in enumerate(
            (
                (touched_h, touched_v), (touched_h, touched_s), (ids_h, ids), (table_h, table_v),
                (w_h, w_v), (w_out_h, w_out), (labels_h, labels), (noise_h, noise),
                (accum_h, accum),
            )
        )
    ]
    for load in loads[:4]:
        load.start()

    barrier = pltpu.get_barrier_semaphore()

    def greet(off, carry):
        pl.semaphore_signal(
            barrier, inc=1, device_id=(g, ahead(off) * 2 + c), device_id_type=MESH
        )
        return carry

    lax.fori_loop(1, 16, greet, 0)
    pl.semaphore_signal(barrier, inc=1, device_id=(g, sib), device_id_type=MESH)
    for i in range(1, 4):
        pl.semaphore_signal(
            barrier, inc=1, device_id=(lax.rem(g + i, 4), t), device_id_type=MESH
        )

    loads[0].wait()
    high_of = lax.broadcasted_iota(jnp.int32, (16, 512), 0)
    low_of = lax.broadcasted_iota(jnp.int32, (128, 512), 0)
    lane = lax.broadcasted_iota(jnp.int32, (1, 512), 1)
    for f in range(4):
        row = touched_v[f : f + 1, :]
        row_low = row & 127
        is_high = high_of == lax.shift_right_logical(row, 7)
        is_low = jnp.where(low_of == row_low, 1.0, 0.0).astype(BF)
        number = jnp.concatenate(
            [
                jnp.where(is_high, lax.shift_right_logical(lane, 4), 0),
                jnp.where(is_high, lane & 15, 0),
            ],
            axis=0,
        )
        pair = split_dot(number.astype(F32).astype(BF), is_low, ((1,), (1,)))
        smap[c * 4 + f] = (pair[:16] * 16.0 + pair[16:]).astype(jnp.int32)
        for q in range(4):
            wide = jnp.broadcast_to(row_low[:, q * 128 : (q + 1) * 128], (128, 128))
            low_col[f, q * 128 : (q + 1) * 128, :] = wide.T

    loads[2].wait()
    for f in range(4):
        for q in range(16):
            to = slice(q * 128, q * 128 + 128)
            ours = pl.ds(pl.multiple_of(q * 256 + c * 128, 128), 128)
            theirs = pl.ds(pl.multiple_of(q * 256 + 128 - c * 128, 128), 128)
            both_ids[c * 4 + f, :, to] = ids[f, :, ours]
            send_ids[f, :, to] = ids[f, :, theirs]

    own_part = pl.ds(c * 4, 4)

    def trade(i):
        source, target = (
            (send_ids, both_ids.at[own_part]),
            (smap.at[own_part], smap.at[own_part]),
            (ttr.at[own_part, pl.ds(0, 128)], ttr.at[own_part, pl.ds(0, 128)]),
        )[i]
        return pltpu.make_async_remote_copy(
            src_ref=source, dst_ref=target, send_sem=s1.at[i], recv_sem=r1.at[i],
            device_id=(g, sib), device_id_type=MESH,
        )

    def traded(i):
        other = pl.ds(4 - c * 4, 4)
        source, target = (
            (send_ids, both_ids.at[other]),
            (smap.at[other], smap.at[other]),
            (ttr.at[other, pl.ds(0, 128)], ttr.at[other, pl.ds(0, 128)]),
        )[i]
        return pltpu.make_async_remote_copy(
            src_ref=source, dst_ref=target, send_sem=s1.at[i], recv_sem=r1.at[i],
            device_id=(g, sib), device_id_type=MESH,
        )

    def pair_ahead(s):
        off = 7 - s
        return lax.rem(y + off // 2, 4) * 4 + lax.rem(x // 2 + lax.rem(off, 2), 2) * 2

    def pair_behind(s):
        off = 7 - s
        return lax.rem(y + 4 - off // 2, 4) * 4 + lax.rem(x // 2 + lax.rem(off, 2), 2) * 2

    sublane = lax.broadcasted_iota(jnp.int32, (8, 128), 0)
    scale = jnp.concatenate([jnp.full((64, 128), 1.0 / scale_of(i), F32) for i in range(8)], axis=0)

    def count(s, f):
        b0 = pl.multiple_of(pair_ahead(s) * 128, 256)
        bag = both_ids[f, :, pl.ds(b0, 256)]
        others = jnp.zeros((8, 256), F32)
        for d in range(1, 5):
            others = others + jnp.where(bag == pltpu.roll(bag, d, 0), 1.0 if d == 4 else 2.0, 0.0)
        slots_of = []
        for half in range(2):
            part = bag[:, half * 128 : half * 128 + 128]
            high = lax.shift_right_logical(part, 7)
            low = part & 127
            slot = jnp.zeros((8, 128), jnp.int32)
            for q in range(16):
                row = jnp.broadcast_to(smap[f, q : q + 1, :], (8, 128))
                slot = jnp.where(high == q, jnp.take_along_axis(row, low, axis=1), slot)
            slots_of.append(slot)
        halves = []
        for slot in slots_of:
            word = slot & 63
            digit = lax.shift_left(
                jnp.ones((8, 128), jnp.int32), lax.shift_right_logical(slot, 6) * 4
            )
            packed = [jnp.zeros((8, 128), jnp.int32) for _ in range(8)]
            for h in range(8):
                place = jnp.broadcast_to(word[h : h + 1], (8, 128)) - sublane
                value = jnp.broadcast_to(digit[h : h + 1], (8, 128))
                for v in range(8):
                    packed[v] = packed[v] + jnp.where(place == 8 * v, value, 0)
            packed = jnp.concatenate(packed, axis=0)
            tiles = []
            for i in range(7):
                tiles.append((packed & (15 << (4 * i))).astype(F32).astype(BF))
            tiles.append(lax.shift_right_logical(packed, 28).astype(F32).astype(BF))
            halves.append(jnp.concatenate(tiles, axis=0))
        block = jnp.concatenate(halves, axis=1)
        bags[s, pl.ds(f, 1), :] = 8.0 + jnp.sum(others, axis=0, keepdims=True)
        ring[f] = block
        counts[f, :, pl.ds(b0, 256)] = block

    def early(n, carry):
        count(0, c * 4 + n)
        return carry

    def early_other(n, carry):
        count(0, 4 - c * 4 + n)
        return carry

    lax.fori_loop(0, 4, early, 0)
    pl.semaphore_wait(barrier, 19)
    trade(0).start()
    trade(1).start()
    loads[1].wait()
    loads[3].wait()
    for load in loads[4:]:
        load.start()

    def pick(n, carry):
        f = n // 16
        k = lax.rem(n, 16) * 32
        for i in range(32):
            r = touched_s[f, k + i]
            trows[f, pl.ds(k + i, 1), :] = table_v[f, pl.ds(r, 1), :]
        return carry

    lax.fori_loop(0, 64, pick, 0)
    for f in range(4):
        ttr[c * 4 + f, 0:128, :] = (trows[f] * scale).T.astype(BF)
    trade(2).start()
    traded(0).wait_recv()
    traded(1).wait_recv()
    lax.fori_loop(0, 4, early_other, 0)
    loads[4].wait()
    traded(2).wait_recv()
    for f in range(8):
        side = w_v[p * 8 + f].astype(F32).T.astype(BF)
        ttr[f, 128:256, :] = split_dot(side, ttr[f, 0:128, :], ((1,), (0,))).astype(BF)

    rows8 = lax.broadcasted_iota(jnp.int32, (8, 256), 0)

    def out_copy(s, half):
        return pltpu.make_async_remote_copy(
            src_ref=outb.at[s * 2 + half], dst_ref=slots.at[p], send_sem=s2.at[s * 2 + half],
            recv_sem=r2.at[p], device_id=(g, (pair_ahead(s) + half) * 2 + c),
            device_id_type=MESH,
        )

    def finish(s, after):
        sumsq = jnp.zeros((1, 256), F32)
        part = jnp.zeros((128, 256), F32)
        for f in range(8):
            both = split_dot(ttr[f], ring[f], ((1,), (0,)))
            pooled = both[:128].astype(BF).astype(F32)
            sumsq = sumsq + jnp.sum(pooled * pooled, axis=0, keepdims=True)
            part = part + both[128:]
            if after is not None:
                count(after, f)
        high = sumsq.astype(BF).astype(F32)
        squares = jnp.where(rows8 == 0, high, 0.0)
        squares = jnp.where(rows8 == 1, sumsq - high, squares)
        extra = jnp.concatenate([bags[s], squares], axis=0)
        for half in range(2):
            lanes_of = slice(half * 128, half * 128 + 128)
            outb[s * 2 + half, 0:128, :] = part[:, lanes_of].astype(BF)
            outb[s * 2 + half, 128:144, :] = extra[:, lanes_of].astype(BF)

    def step(s, carry):
        finish(s, s + 1)
        out_copy(s, 0).start()
        out_copy(s, 1).start()
        return carry

    lax.fori_loop(0, 7, step, 0)
    finish(7, None)
    odd = lax.rem(x, 2)
    out_copy(7, 1 - odd).start()
    slots[p] = outb[14 + odd]
    for f in range(8):
        s_acc[f] = jnp.zeros((512, 128), F32)

    pacc[...] = slots[p, 0:128, :].astype(F32)

    def from_chip(src):
        pltpu.make_async_remote_copy(
            src_ref=outb.at[0], dst_ref=slots.at[src], send_sem=s2.at[0], recv_sem=r2.at[src],
            device_id=(g, sib), device_id_type=MESH,
        ).wait_recv()
        pacc[...] += slots[src, 0:128, :].astype(F32)

    def arrive(s, carry):
        from_chip(pair_behind(s))
        from_chip(pair_behind(s) + 1)
        return carry

    lax.fori_loop(0, 7, arrive, 0)
    from_chip(p + 1 - 2 * odd)
    loads[5].wait()
    loads[6].wait()
    pre = pacc[...]
    weight = jnp.broadcast_to(w_out[...], (128, 128)).T
    gate = jax.nn.sigmoid(pre)
    logit = jnp.sum(pre * gate * weight, axis=0, keepdims=True)
    prob = jax.nn.sigmoid(logit)
    delta = gate * (1.0 + pre * (1.0 - gate)) * weight * (prob - labels[...])
    delta_low = delta.astype(BF)

    nothing = jnp.zeros((128, 128), BF)
    twice = jnp.concatenate(
        [
            jnp.concatenate([delta_low, nothing], axis=1),
            jnp.concatenate([nothing, delta_low], axis=1),
        ],
        axis=0,
    )

    def norms(q, carry):
        acc, ssq = carry
        weights = w_v[pl.ds(q * 32, 32)]
        side = jnp.concatenate(
            [weights[:16].reshape(2048, 128), weights[16:].reshape(2048, 128)], axis=1
        )
        grad = split_dot(side, twice, ((1,), (0,)))
        square = jnp.sum((grad * grad).reshape(16, 128, 256), axis=1)
        for i in range(4):
            tail = slots[q * 4 + i, 128:144, :].astype(F32)
            half = square[:, :128] if i < 2 else square[:, 128:]
            acc = acc + half[(i % 2) * 8 : (i % 2) * 8 + 8] * tail[0:8]
            ssq = ssq + tail[8:16]
        return acc, ssq

    acc, ssq = lax.fori_loop(
        0, 4, norms, (jnp.zeros((8, 128), F32), jnp.zeros((8, 128), F32))
    )
    norm_sq = jnp.sum(acc, axis=0, keepdims=True) + jnp.sum(
        ssq, axis=0, keepdims=True
    ) * jnp.sum(delta * delta, axis=0, keepdims=True)
    factor = CLIP / jnp.maximum(jnp.sqrt(norm_sq), CLIP)
    clip[p] = (factor * delta).T.astype(BF)

    def high_one(f):
        row = lax.shift_right_logical(touched_v[pl.ds(f, 1), :], 7)
        return jnp.where(high_of == row, 1.0, 0.0).astype(BF)

    def three(values):
        first = values.astype(BF)
        rest = values - first.astype(F32)
        second = rest.astype(BF)
        return first, second, (rest - second.astype(F32)).astype(BF)

    def nth(table, n):
        packed = sum(v << (4 * i) for i, v in enumerate(table))
        packed = packed - (1 << 32) if packed >= 1 << 31 else packed
        return lax.shift_right_logical(jnp.int32(packed), 4 * n) & 15

    def offsets(n):
        return nth((0, 3, 12, 15, 13, 8, 9, 11), n), nth((1, 4, 5, 7, 2, 6, 14, 10), n)

    def clip_copy(off, src):
        return pltpu.make_async_remote_copy(
            src_ref=clip.at[src], dst_ref=clip.at[src], send_sem=s3.at[off],
            recv_sem=r3.at[src], device_id=(g, ahead(off) * 2 + c), device_id_type=MESH,
        )

    def spread(n, carry):
        for off in offsets(n):
            clip_copy(off, p).start()
        return carry

    clip_copy(1, p).start()
    lax.fori_loop(1, 8, spread, 0)

    lanes = lax.broadcasted_iota(jnp.int32, (512, 128), 1)
    loads[8].wait()
    for f in range(4):
        is_high = high_one(f)
        values = jnp.concatenate(
            [accum[f : f + 1, q * 128 : (q + 1) * 128] for q in range(16)], axis=0
        )
        first, second, third = three(values)
        spread_out = split_dot(
            jnp.concatenate([is_high, is_high, is_high], axis=0),
            jnp.concatenate([first, second, third], axis=0),
            ((0,), (0,)),
        )
        found = jnp.where(lanes == low_col[f], spread_out, 0.0)
        accb[f] = jnp.broadcast_to(jnp.sum(found, axis=1, keepdims=True), (512, 128))

    def product(f, n):
        chips = [behind(off) for off in offsets(n)]
        side = [counts[f, :, pl.ds(pl.multiple_of(q * 128, 128), 128)] for q in chips]
        rows = [clip[q] for q in chips]
        return split_dot(
            jnp.concatenate(side, axis=1), jnp.concatenate(rows, axis=0), ((1,), (0,))
        )

    def arrived(off):
        clip_copy(off, behind(off)).wait_recv()

    def drain(s, carry):
        out_copy(s, 0).wait_send()
        out_copy(s, 1).wait_send()
        return carry

    lax.fori_loop(0, 7, drain, 0)
    out_copy(7, 1 - odd).wait_send()
    for i in range(3):
        trade(i).wait_send()

    def gather(n, carry):
        for f in range(8):
            s_acc[f] += product(f, n - 1)
        for off in offsets(n):
            arrived(off)
        return carry

    arrived(1)
    lax.fori_loop(1, 8, gather, 0)

    def half_copy(i):
        return pltpu.make_async_remote_copy(
            src_ref=half_send.at[i], dst_ref=half_recv.at[i], send_sem=s4.at[i],
            recv_sem=r4.at[i], device_id=(g, sib), device_id_type=MESH,
        )

    def other_features(i, carry):
        f = 4 - c * 4 + lax.rem(g + 1 + i, 4)
        half_send[i] = ((s_acc[f] + product(f, 7)) * scale).astype(BF)
        half_copy(i).start()
        return carry

    lax.fori_loop(0, 4, other_features, 0)

    def own_features(i, carry):
        to = lax.rem(g + 1 + i, 4)
        f = c * 4 + to
        part = (s_acc[f] + product(f, 7)) * scale
        half_copy(i).wait_recv()
        part = part + half_recv[i].astype(F32)
        s_acc[f] = part

        @pl.when(i < 3)
        def _():
            zsend[i] = part.astype(BF)
            pltpu.make_async_remote_copy(
                src_ref=zsend.at[i], dst_ref=zrecv.at[g], send_sem=s5.at[i],
                recv_sem=r5.at[g], device_id=(to, t), device_id_type=MESH,
            ).start()

        return carry

    lax.fori_loop(0, 4, own_features, 0)

    def drain_far(off, carry):
        clip_copy(off, p).wait_send()
        return carry

    lax.fori_loop(1, 16, drain_far, 0)
    for i in range(4):
        half_copy(i).wait_send()
    summed = s_acc[c * 4 + g]
    for i in range(3):
        src = lax.rem(g + 3 - i, 4)
        pltpu.make_async_remote_copy(
            src_ref=zsend.at[i], dst_ref=zrecv.at[src], send_sem=s5.at[i], recv_sem=r5.at[src],
            device_id=(lax.rem(g + 1 + i, 4), t), device_id_type=MESH,
        ).wait_recv()
        summed = summed + zrecv[src].astype(F32)
    low = summed.astype(BF)
    rg[g] = split_dot(low, w_v[t * 4 + g], ((1,), (1,))).astype(BF)

    def row_copy(i):
        return pltpu.make_async_remote_copy(
            src_ref=rg.at[g], dst_ref=rg.at[g], send_sem=s6.at[i], recv_sem=r6.at[g],
            device_id=(lax.rem(g + 1 + i, 4), t), device_id_type=MESH,
        )

    def dense_copy(i):
        to = lax.rem(g + 1 + i, 4)
        return pltpu.make_async_remote_copy(
            src_ref=dsend.at[to], dst_ref=dense_v.at[g], send_sem=s7.at[i], recv_sem=r7.at[g],
            device_id=(to, t), device_id_type=MESH,
        )

    for i in range(3):
        row_copy(i).start()
    dsend[...] = split_dot(trows[g].T.astype(BF), low, ((1,), (0,))).reshape(4, 32, 128)
    for i in range(3):
        dense_copy(i).start()
    dense_v[g] = dsend[g]

    def rows_save(f):
        return pltpu.make_async_copy(rows_v.at[f], rows_out.at[f], out_sem.at[f])

    def update(f):
        listed = rg[f].astype(F32) + noise[f]
        mean = jnp.sum(listed * listed, axis=1, keepdims=True) * (1.0 / 128.0)
        new_acc = accb[f] + mean
        rows_v[f] = trows[f] - LEARN * listed / jnp.sqrt(new_acc)
        is_high = high_one(f)
        first, second, third = three(jnp.where(lanes == low_col[f], mean, 0.0))
        macc_v[f] = (
            split_dot(is_high, first, ((1,), (0,)))
            + split_dot(is_high, second, ((1,), (0,)))
            + split_dot(is_high, third, ((1,), (0,)))
        )
        rows_save(f).start()

    loads[7].wait()
    update(g)
    for i in range(3):
        src = lax.rem(g + 3 - i, 4)
        pltpu.make_async_remote_copy(
            src_ref=rg.at[g], dst_ref=rg.at[src], send_sem=s6.at[i], recv_sem=r6.at[src],
            device_id=(lax.rem(g + 1 + i, 4), t), device_id_type=MESH,
        ).wait_recv()
        update(src)
    for i in range(3):
        src = lax.rem(g + 3 - i, 4)
        pltpu.make_async_remote_copy(
            src_ref=dsend.at[0], dst_ref=dense_v.at[src], send_sem=s7.at[i],
            recv_sem=r7.at[src], device_id=(lax.rem(g + 1 + i, 4), t), device_id_type=MESH,
        ).wait_recv()

    saves = [
        pltpu.make_async_copy(macc_v, macc_out, out_sem.at[4]),
        pltpu.make_async_copy(dense_v, dense_out, out_sem.at[5]),
    ]
    for save in saves:
        save.start()

    for i in range(3):
        pltpu.make_async_remote_copy(
            src_ref=zsend.at[i], dst_ref=zrecv.at[g], send_sem=s5.at[i], recv_sem=r5.at[g],
            device_id=(lax.rem(g + 1 + i, 4), t), device_id_type=MESH,
        ).wait_send()
        row_copy(i).wait_send()
        dense_copy(i).wait_send()
    for f in range(4):
        rows_save(f).wait()
    for save in saves:
        save.wait()


def write_rows(
    touched_h, accum_h, macc_h, dense_h, noise_h, table_h, rows_h,
    table_out, accum_out, dense_out,
    touched_s, accum, macc, dense, noise, block, rows, sem, in_sem, rows_sem, out_sem,
):
    def load(f):
        return pltpu.make_async_copy(table_h.at[f], block.at[f], in_sem.at[f])

    def load_rows(f):
        return pltpu.make_async_copy(rows_h.at[f], rows.at[f], rows_sem.at[f])

    def save(f):
        return pltpu.make_async_copy(block.at[f], table_out.at[f], out_sem.at[f])

    load(0).start()
    load_rows(0).start()
    small = [
        pltpu.make_async_copy(source, target, sem.at[i])
        for i, (source, target) in enumerate(
            (
                (touched_h, touched_s), (accum_h, accum), (macc_h, macc),
                (dense_h, dense), (noise_h, noise),
            )
        )
    ]
    for copy in small:
        copy.start()
    for f in range(1, 4):
        load(f).start()
        load_rows(f).start()
    for copy in small:
        copy.wait()
    dense[...] += noise[...]
    save_dense = pltpu.make_async_copy(dense, dense_out, sem.at[5])
    save_dense.start()
    for f in range(4):
        for q in range(16):
            lanes = slice(q * 128, (q + 1) * 128)
            accum[f : f + 1, lanes] += macc[f, q : q + 1, :]
    save_accum = pltpu.make_async_copy(accum, accum_out, sem.at[6])
    save_accum.start()
    for f in range(4):
        load(f).wait()
        load_rows(f).wait()

        def put(n, carry):
            k = pl.multiple_of(n * 64, 64)
            for i in range(64):
                block[f, pl.ds(touched_s[f, k + i], 1), :] = rows[f, pl.ds(k + i, 1), :]
            return carry

        lax.fori_loop(0, 8, put, 0)
        save(f).start()
    save_dense.wait()
    save_accum.wait()
    for f in range(4):
        save(f).wait()


def body(table, accum, w_hidden, w_out, ids, labels, touched, row_noise, dense_noise):
    hbm = pl.BlockSpec(memory_space=pl.ANY)
    dma = pltpu.SemaphoreType.DMA
    rows, macc, dense = pl.pallas_call(
        core,
        out_shape=(
            jax.ShapeDtypeStruct((4, 512, 128), F32),
            jax.ShapeDtypeStruct((4, 16, 128), F32),
            jax.ShapeDtypeStruct((4, 32, 128), F32),
        ),
        in_specs=[hbm] * 8,
        out_specs=(hbm, hbm, hbm),
        scratch_shapes=[
            pltpu.SMEM((4, 512), jnp.int32),
            pltpu.VMEM((4, 512), jnp.int32),
            pltpu.VMEM((4, 2048), F32),
            pltpu.VMEM((4, 8, 4096), jnp.int32),
            pltpu.VMEM((1, 128), F32),
            pltpu.VMEM((1, 128), F32),
            pltpu.VMEM((4, 512, 128), F32),
            pltpu.VMEM((4, 512, 128), F32),
            pltpu.VMEM((4, 16, 128), F32),
            pltpu.VMEM((4, 32, 128), F32),
            pltpu.VMEM((4, 2048, 128), F32),
            pltpu.VMEM((128, 128, 128), BF),
            pltpu.VMEM((4, 512, 128), F32),
            pltpu.VMEM((8, 256, 512), BF),
            pltpu.VMEM((8, 16, 128), jnp.int32),
            pltpu.VMEM((4, 512, 128), jnp.int32),
            pltpu.VMEM((8, 512, 2048), BF),
            pltpu.VMEM((8, 512, 256), BF),
            pltpu.VMEM((8, 8, 256), F32),
            pltpu.VMEM((8, 8, 2048), jnp.int32),
            pltpu.VMEM((4, 8, 2048), jnp.int32),
            pltpu.VMEM((16, 144, 128), BF),
            pltpu.VMEM((16, 144, 128), BF),
            pltpu.VMEM((128, 128), F32),
            pltpu.VMEM((16, 128, 128), BF),
            pltpu.VMEM((4, 512, 128), F32),
            pltpu.VMEM((8, 512, 128), F32),
            pltpu.VMEM((4, 512, 128), BF),
            pltpu.VMEM((4, 512, 128), BF),
            pltpu.VMEM((3, 512, 128), BF),
            pltpu.VMEM((4, 512, 128), BF),
            pltpu.VMEM((4, 512, 128), BF),
            pltpu.VMEM((4, 32, 128), F32),
            dma((9,)),
            dma((3,)), dma((3,)), dma((16,)), dma((16,)), dma((16,)), dma((16,)),
            dma((4,)), dma((4,)),
            dma((3,)), dma((4,)), dma((3,)), dma((4,)), dma((3,)), dma((4,)),
            dma((6,)),
        ],
        compiler_params=pltpu.CompilerParams(
            collective_id=0, has_side_effects=True, vmem_limit_bytes=56 * 1024 * 1024
        ),
        cost_estimate=pl.CostEstimate(
            flops=6 * 10**9, bytes_accessed=12 * 2**20, transcendentals=10**5
        ),
        name="step",
    )(
        touched, accum, ids, w_out.reshape(1, 128), labels.reshape(1, 128),
        row_noise, table, w_hidden,
    )
    return pl.pallas_call(
        write_rows,
        out_shape=(
            jax.ShapeDtypeStruct((4, 2048, 128), F32),
            jax.ShapeDtypeStruct((4, 2048), F32),
            jax.ShapeDtypeStruct((4, 32, 128), F32),
        ),
        in_specs=[hbm] * 7,
        out_specs=(hbm, hbm, hbm),
        scratch_shapes=[
            pltpu.SMEM((4, 512), jnp.int32),
            pltpu.VMEM((4, 2048), F32),
            pltpu.VMEM((4, 16, 128), F32),
            pltpu.VMEM((4, 32, 128), F32),
            pltpu.VMEM((4, 32, 128), F32),
            pltpu.VMEM((4, 2048, 128), F32),
            pltpu.VMEM((4, 512, 128), F32),
            dma((7,)), dma((4,)), dma((4,)), dma((4,)),
        ],
        compiler_params=pltpu.CompilerParams(vmem_limit_bytes=60 * 1024 * 1024),
        name="write_rows",
    )(touched, accum, macc, dense, dense_noise, table, rows)


def solution(mesh):
    in_specs = (
        P("table", None, None),
        P("table", None),
        P(),
        P(),
        P("table", None, "group"),
        P(("group", "table")),
        P("table", None),
        P("table", None, None),
        P("table", "group", None),
    )
    out_specs = (P("table", None, None), P("table", None), P("table", "group", None))
    return jax.shard_map(body, mesh=mesh, in_specs=in_specs, out_specs=out_specs, check_vma=False)
```

time: 77.4 us -> 74.7 us (0.965)
  Pallas kernels: 76.7 us -> 73.8 us
    pallas_call x1, Pallas kernels: 69.1 us -> 66.3 us  [body(): pl.pallas_call(core, out_shape=(jax.ShapeDtypeStruct((4, 512, 128), F32),...]
where the time goes in v4:
time: 74.7 us; the launch traced here: 74.5 us
  Pallas kernels  73.8 us (99%)
    pallas_call x1, Pallas kernels, body(): pl.pallas_call(core, out_shape=(jax.ShapeDtypeStruct((4, 512, 128), F32),...  66.3 us
    pallas_call x1, Pallas kernels, body(): pl.pallas_call(write_rows, out_shape=(jax.ShapeDtypeStruct((4, 2048, 128)...  7.59 us

profile of v4, /device:TPU:0, one launch (start us, length us, event | category | flops | bytes accessed | tf_op | source)
XLA Modules:
  0.0 74.5 jit_solution(8513704868532744048)
XLA Ops:
  0.6 66.3 %step.1 = (f32[4,512,128]{2,1,0:T(8,128)}, f32[4,16,128]{2,1,0:T(8,128)}, f32[4,32,128]{2,1,0:T(8,128)}) custom-call(s32[4,512]{1,0:T(4,128)} %touched_h.3, f32[4,2048]{1,0:T(4,128)} %accum_h.3, s32[4,8,4096]{2,1,0:T(8,128)} %ids_h.1, f32[1,128]{1,0:T(1,128)} %bitcast.2, f32[1,128]{1,0:T(1,128)} %bitcast.3, f32[4,512,128]{2,1,0:T(8,128)} %noise_h.2, ...), custom_call_target="tpu_custom_call" | custom-call | flops 6000000000 | bytes 12582912 | tf_op jit(solution)/shard_map/step/pallas_call | solution.py:586
  66.9 7.6 %write_rows.1 = (f32[4,2048,128]{2,1,0:T(8,128)}, f32[4,2048]{1,0:T(4,128)}, f32[4,32,128]{2,1,0:T(8,128)}) custom-call(s32[4,512]{1,0:T(4,128)} %touched_h.3, f32[4,2048]{1,0:T(4,128)} %accum_h.3, f32[4,16,128]{2,1,0:T(8,128)} %get-tuple-element.6.macc_h, f32[4,32,128]{2,1,0:T(8,128)} %get-tuple-element.7.dense_h, f32[4,32,128]{2,1,0:T(8,128)} %noise_h.3, ...), custom_call_target="tpu_custom_call" | custom-call | tf_op jit(solution)/shard_map/write_rows/pallas_call | solution.py:646

commit v5 on v4

--- a/solution.py
+++ b/solution.py
@@ -365,12 +365,14 @@
         found = jnp.where(lanes == low_col[f], spread_out, 0.0)
         accb[f] = jnp.broadcast_to(jnp.sum(found, axis=1, keepdims=True), (512, 128))
 
-    def product(f, n):
+    def product(f, n, first=0, rows=512):
         chips = [behind(off) for off in offsets(n)]
-        side = [counts[f, :, pl.ds(pl.multiple_of(q * 128, 128), 128)] for q in chips]
-        rows = [clip[q] for q in chips]
+        side = [
+            counts[f, first : first + rows, pl.ds(pl.multiple_of(q * 128, 128), 128)] for q in chips
+        ]
+        blocks = [clip[q] for q in chips]
         return split_dot(
-            jnp.concatenate(side, axis=1), jnp.concatenate(rows, axis=0), ((1,), (0,))
+            jnp.concatenate(side, axis=1), jnp.concatenate(blocks, axis=0), ((1,), (0,))
         )
 
     def arrived(off):
@@ -396,127 +398,141 @@
     arrived(1)
     lax.fori_loop(1, 8, gather, 0)
 
-    def half_copy(i):
-        return pltpu.make_async_remote_copy(
-            src_ref=half_send.at[i], dst_ref=half_recv.at[i], send_sem=s4.at[i],
-            recv_sem=r4.at[i], device_id=(g, sib), device_id_type=MESH,
-        )
-
-    def other_features(i, carry):
-        f = 4 - c * 4 + lax.rem(g + 1 + i, 4)
-        half_send[i] = ((s_acc[f] + product(f, 7)) * scale).astype(BF)
-        half_copy(i).start()
-        return carry
-
-    lax.fori_loop(0, 4, other_features, 0)
-
-    def own_features(i, carry):
+    def piece(part):
+        return pl.ds(part * 256, 256)
+
+    def half_copy(part, i):
+        return pltpu.make_async_remote_copy(
+            src_ref=half_send.at[i, piece(part)], dst_ref=half_recv.at[i, piece(part)],
+            send_sem=s4.at[part * 4 + i], recv_sem=r4.at[part * 4 + i],
+            device_id=(g, sib), device_id_type=MESH,
+        )
+
+    def sum_copy(part, i, src):
+        return pltpu.make_async_remote_copy(
+            src_ref=zsend.at[i, piece(part)], dst_ref=zrecv.at[src, piece(part)],
+            send_sem=s5.at[part * 3 + i], recv_sem=r5.at[part * 4 + src],
+            device_id=(lax.rem(g + 1 + i, 4), t), device_id_type=MESH,
+        )
+
+    def row_copy(part, i, src):
+        return pltpu.make_async_remote_copy(
+            src_ref=rg.at[src, piece(part)], dst_ref=rg.at[src, piece(part)],
+            send_sem=s6.at[part * 3 + i], recv_sem=r6.at[part * 4 + src],
+            device_id=(lax.rem(g + 1 + i, 4), t), device_id_type=MESH,
+        )
+
+    def dense_copy(i, src):
         to = lax.rem(g + 1 + i, 4)
-        f = c * 4 + to
-        part = (s_acc[f] + product(f, 7)) * scale
-        half_copy(i).wait_recv()
-        part = part + half_recv[i].astype(F32)
-        s_acc[f] = part
-
-        @pl.when(i < 3)
-        def _():
-            zsend[i] = part.astype(BF)
-            pltpu.make_async_remote_copy(
-                src_ref=zsend.at[i], dst_ref=zrecv.at[g], send_sem=s5.at[i],
-                recv_sem=r5.at[g], device_id=(to, t), device_id_type=MESH,
-            ).start()
-
-        return carry
-
-    lax.fori_loop(0, 4, own_features, 0)
+        return pltpu.make_async_remote_copy(
+            src_ref=dsend.at[to], dst_ref=dense_v.at[src], send_sem=s7.at[i],
+            recv_sem=r7.at[src], device_id=(to, t), device_id_type=MESH,
+        )
+
+    def source(i):
+        return lax.rem(g + 3 - i, 4)
+
+    def rows_sum(f, part):
+        rows = slice(part * 256, part * 256 + 256)
+        return (s_acc[f, rows] + product(f, 7, part * 256, 256)) * scale[rows]
+
+    for part in range(2):
+
+        def other_features(i, carry):
+            f = 4 - c * 4 + lax.rem(g + 1 + i, 4)
+            half_send[i, piece(part)] = rows_sum(f, part).astype(BF)
+            half_copy(part, i).start()
+            return carry
+
+        lax.fori_loop(0, 4, other_features, 0)
+
+    for part in range(2):
+
+        def own_features(i, carry):
+            f = c * 4 + lax.rem(g + 1 + i, 4)
+            total = rows_sum(f, part)
+            half_copy(part, i).wait_recv()
+            total = total + half_recv[i, piece(part)].astype(F32)
+            s_acc[f, piece(part)] = total
+
+            @pl.when(i < 3)
+            def _():
+                zsend[i, piece(part)] = total.astype(BF)
+                sum_copy(part, i, g).start()
+
+            return carry
+
+        lax.fori_loop(0, 4, own_features, 0)
 
     def drain_far(off, carry):
         clip_copy(off, p).wait_send()
         return carry
 
     lax.fori_loop(1, 16, drain_far, 0)
-    for i in range(4):
-        half_copy(i).wait_send()
-    summed = s_acc[c * 4 + g]
+    for part in range(2):
+        for i in range(4):
+            half_copy(part, i).wait_send()
+
+    side = trows[g].T.astype(BF)
+    dense_sum = jnp.zeros((128, 128), F32)
+    for part in range(2):
+        summed = s_acc[c * 4 + g, piece(part)]
+        for i in range(3):
+            sum_copy(part, i, source(i)).wait_recv()
+            summed = summed + zrecv[source(i), piece(part)].astype(F32)
+        low = summed.astype(BF)
+        rg[g, piece(part)] = split_dot(low, w_v[t * 4 + g], ((1,), (1,))).astype(BF)
+        for i in range(3):
+            row_copy(part, i, g).start()
+        dense_sum = dense_sum + split_dot(
+            side[:, part * 256 : part * 256 + 256], low, ((1,), (0,))
+        )
+    dsend[...] = dense_sum.reshape(4, 32, 128)
     for i in range(3):
-        src = lax.rem(g + 3 - i, 4)
-        pltpu.make_async_remote_copy(
-            src_ref=zsend.at[i], dst_ref=zrecv.at[src], send_sem=s5.at[i], recv_sem=r5.at[src],
-            device_id=(lax.rem(g + 1 + i, 4), t), device_id_type=MESH,
-        ).wait_recv()
-        summed = summed + zrecv[src].astype(F32)
-    low = summed.astype(BF)
-    rg[g] = split_dot(low, w_v[t * 4 + g], ((1,), (1,))).astype(BF)
-
-    def row_copy(i):
-        return pltpu.make_async_remote_copy(
-            src_ref=rg.at[g], dst_ref=rg.at[g], send_sem=s6.at[i], recv_sem=r6.at[g],
-            device_id=(lax.rem(g + 1 + i, 4), t), device_id_type=MESH,
-        )
-
-    def dense_copy(i):
-        to = lax.rem(g + 1 + i, 4)
-        return pltpu.make_async_remote_copy(
-            src_ref=dsend.at[to], dst_ref=dense_v.at[g], send_sem=s7.at[i], recv_sem=r7.at[g],
-            device_id=(to, t), device_id_type=MESH,
-        )
-
+        dense_copy(i, g).start()
+    dense_v[g] = dsend[g]
+
+    def rows_save(f, part):
+        return pltpu.make_async_copy(
+            rows_v.at[f, piece(part)], rows_out.at[f, piece(part)], out_sem.at[part * 4 + f]
+        )
+
+    def update(f, part):
+        rows = slice(part * 256, part * 256 + 256)
+        listed = rg[f, rows].astype(F32) + noise[f, rows]
+        mean = jnp.sum(listed * listed, axis=1, keepdims=True) * (1.0 / 128.0)
+        new_acc = accb[f, rows] + mean
+        rows_v[f, rows] = trows[f, rows] - LEARN * listed / jnp.sqrt(new_acc)
+        rows_save(f, part).start()
+        is_high = high_one(f)[:, rows]
+        added = jnp.zeros((16, 128), F32)
+        for one in three(jnp.where(lanes[rows] == low_col[f, rows], mean, 0.0)):
+            added = added + split_dot(is_high, one, ((1,), (0,)))
+        macc_v[f] = added if part == 0 else macc_v[f] + added
+
+    loads[7].wait()
+    for part in range(2):
+        update(g, part)
+        for i in range(3):
+            row_copy(part, i, source(i)).wait_recv()
+            update(source(i), part)
     for i in range(3):
-        row_copy(i).start()
-    dsend[...] = split_dot(trows[g].T.astype(BF), low, ((1,), (0,))).reshape(4, 32, 128)
-    for i in range(3):
-        dense_copy(i).start()
-    dense_v[g] = dsend[g]
-
-    def rows_save(f):
-        return pltpu.make_async_copy(rows_v.at[f], rows_out.at[f], out_sem.at[f])
-
-    def update(f):
-        listed = rg[f].astype(F32) + noise[f]
-        mean = jnp.sum(listed * listed, axis=1, keepdims=True) * (1.0 / 128.0)
-        new_acc = accb[f] + mean
-        rows_v[f] = trows[f] - LEARN * listed / jnp.sqrt(new_acc)
-        is_high = high_one(f)
-        first, second, third = three(jnp.where(lanes == low_col[f], mean, 0.0))
-        macc_v[f] = (
-            split_dot(is_high, first, ((1,), (0,)))
-            + split_dot(is_high, second, ((1,), (0,)))
-            + split_dot(is_high, third, ((1,), (0,)))
-        )
-        rows_save(f).start()
-
-    loads[7].wait()
-    update(g)
-    for i in range(3):
-        src = lax.rem(g + 3 - i, 4)
-        pltpu.make_async_remote_copy(
-            src_ref=rg.at[g], dst_ref=rg.at[src], send_sem=s6.at[i], recv_sem=r6.at[src],
-            device_id=(lax.rem(g + 1 + i, 4), t), device_id_type=MESH,
-        ).wait_recv()
-        update(src)
-    for i in range(3):
-        src = lax.rem(g + 3 - i, 4)
-        pltpu.make_async_remote_copy(
-            src_ref=dsend.at[0], dst_ref=dense_v.at[src], send_sem=s7.at[i],
-            recv_sem=r7.at[src], device_id=(lax.rem(g + 1 + i, 4), t), device_id_type=MESH,
-        ).wait_recv()
-
+        dense_copy(i, source(i)).wait_recv()
     saves = [
-        pltpu.make_async_copy(macc_v, macc_out, out_sem.at[4]),
-        pltpu.make_async_copy(dense_v, dense_out, out_sem.at[5]),
+        pltpu.make_async_copy(macc_v, macc_out, out_sem.at[8]),
+        pltpu.make_async_copy(dense_v, dense_out, out_sem.at[9]),
     ]
     for save in saves:
         save.start()
-
+    for part in range(2):
+        for i in range(3):
+            sum_copy(part, i, g).wait_send()
+            row_copy(part, i, g).wait_send()
     for i in range(3):
-        pltpu.make_async_remote_copy(
-            src_ref=zsend.at[i], dst_ref=zrecv.at[g], send_sem=s5.at[i], recv_sem=r5.at[g],
-            device_id=(lax.rem(g + 1 + i, 4), t), device_id_type=MESH,
-        ).wait_send()
-        row_copy(i).wait_send()
-        dense_copy(i).wait_send()
-    for f in range(4):
-        rows_save(f).wait()
+        dense_copy(i, g).wait_send()
+    for part in range(2):
+        for f in range(4):
+            rows_save(f, part).wait()
     for save in saves:
         save.wait()
 
@@ -628,9 +644,9 @@
             pltpu.VMEM((4, 32, 128), F32),
             dma((9,)),
             dma((3,)), dma((3,)), dma((16,)), dma((16,)), dma((16,)), dma((16,)),
-            dma((4,)), dma((4,)),
-            dma((3,)), dma((4,)), dma((3,)), dma((4,)), dma((3,)), dma((4,)),
-            dma((6,)),
+            dma((8,)), dma((8,)),
+            dma((6,)), dma((8,)), dma((6,)), dma((8,)), dma((3,)), dma((4,)),
+            dma((10,)),
         ],
         compiler_params=pltpu.CompilerParams(
             collective_id=0, has_side_effects=True, vmem_limit_bytes=56 * 1024 * 1024

time: 74.7 us -> 72 us (0.964)
  Pallas kernels: 73.8 us -> 71.1 us
    pallas_call x1, Pallas kernels: 66.3 us -> 63.5 us  [body(): pl.pallas_call(core, out_shape=(jax.ShapeDtypeStruct((4, 512, 128), F32),...]
where the time goes in v5:
time: 72 us; the launch traced here: 71.8 us
  Pallas kernels  71.1 us (99%)
    pallas_call x1, Pallas kernels, body(): pl.pallas_call(core, out_shape=(jax.ShapeDtypeStruct((4, 512, 128), F32),...  63.5 us
    pallas_call x1, Pallas kernels, body(): pl.pallas_call(write_rows, out_shape=(jax.ShapeDtypeStruct((4, 2048, 128)...  7.59 us

profile of v5, /device:TPU:0, one launch (start us, length us, event | category | flops | bytes accessed | tf_op | source)
XLA Modules:
  0.0 71.8 jit_solution(10141802819270142538)
XLA Ops:
  0.6 63.5 %step.1 = (f32[4,512,128]{2,1,0:T(8,128)}, f32[4,16,128]{2,1,0:T(8,128)}, f32[4,32,128]{2,1,0:T(8,128)}) custom-call(s32[4,512]{1,0:T(4,128)} %touched_h.3, f32[4,2048]{1,0:T(4,128)} %accum_h.3, s32[4,8,4096]{2,1,0:T(8,128)} %ids_h.1, f32[1,128]{1,0:T(1,128)} %bitcast.2, f32[1,128]{1,0:T(1,128)} %bitcast.3, f32[4,512,128]{2,1,0:T(8,128)} %noise_h.2, ...), custom_call_target="tpu_custom_call" | custom-call | flops 6000000000 | bytes 12582912 | tf_op jit(solution)/shard_map/step/pallas_call | solution.py:602
  64.2 7.6 %write_rows.1 = (f32[4,2048,128]{2,1,0:T(8,128)}, f32[4,2048]{1,0:T(4,128)}, f32[4,32,128]{2,1,0:T(8,128)}) custom-call(s32[4,512]{1,0:T(4,128)} %touched_h.3, f32[4,2048]{1,0:T(4,128)} %accum_h.3, f32[4,16,128]{2,1,0:T(8,128)} %get-tuple-element.6.macc_h, f32[4,32,128]{2,1,0:T(8,128)} %get-tuple-element.7.dense_h, f32[4,32,128]{2,1,0:T(8,128)} %noise_h.3, ...), custom_call_target="tpu_custom_call" | custom-call | tf_op jit(solution)/shard_map/write_rows/pallas_call | solution.py:662

commit v6 on v5

--- a/solution.py
+++ b/solution.py
@@ -48,13 +48,17 @@
         pltpu.make_async_copy(source, target, load_sem.at[i])
         for i, (source, target) in enumerate(
             (
-                (touched_h, touched_v), (touched_h, touched_s), (ids_h, ids), (table_h, table_v),
+                (touched_h, touched_v), (touched_h.at[0], touched_s.at[pl.ds(0, 512)]),
+                (ids_h, ids), (table_h, table_v),
                 (w_h, w_v), (w_out_h, w_out), (labels_h, labels), (noise_h, noise),
                 (accum_h, accum),
+                (touched_h.at[1], touched_s.at[pl.ds(512, 512)]),
+                (touched_h.at[2], touched_s.at[pl.ds(1024, 512)]),
+                (touched_h.at[3], touched_s.at[pl.ds(1536, 512)]),
             )
         )
     ]
-    for load in loads[:4]:
+    for load in loads[:4] + loads[9:]:
         load.start()
 
     barrier = pltpu.get_barrier_semaphore()
@@ -89,7 +93,13 @@
             axis=0,
         )
         pair = split_dot(number.astype(F32).astype(BF), is_low, ((1,), (1,)))
-        smap[c * 4 + f] = (pair[:16] * 16.0 + pair[16:]).astype(jnp.int32)
+        place = (pair[:16] * 16.0 + pair[16:]).astype(jnp.int32)
+        for j in range(6):
+            word = place[3 * j : 3 * j + 1]
+            for i in range(1, min(3, 16 - 3 * j)):
+                word = word | lax.shift_left(place[3 * j + i : 3 * j + i + 1], 9 * i)
+            smap[c * 4 + f, j : j + 1, :] = word
+        smap[c * 4 + f, 6:8, :] = jnp.zeros((2, 128), jnp.int32)
         for q in range(4):
             wide = jnp.broadcast_to(row_low[:, q * 128 : (q + 1) * 128], (128, 128))
             low_col[f, q * 128 : (q + 1) * 128, :] = wide.T
@@ -150,11 +160,12 @@
             part = bag[:, half * 128 : half * 128 + 128]
             high = lax.shift_right_logical(part, 7)
             low = part & 127
-            slot = jnp.zeros((8, 128), jnp.int32)
-            for q in range(16):
+            third = lax.shift_right_logical(high * 11, 5)
+            found = jnp.zeros((8, 128), jnp.int32)
+            for q in range(6):
                 row = jnp.broadcast_to(smap[f, q : q + 1, :], (8, 128))
-                slot = jnp.where(high == q, jnp.take_along_axis(row, low, axis=1), slot)
-            slots_of.append(slot)
+                found = jnp.where(third == q, jnp.take_along_axis(row, low, axis=1), found)
+            slots_of.append(lax.shift_right_logical(found, (high - third * 3) * 9) & 511)
         halves = []
         for slot in slots_of:
             word = slot & 63
@@ -192,29 +203,37 @@
     trade(1).start()
     loads[1].wait()
     loads[3].wait()
-    for load in loads[4:]:
+    for load in loads[9:]:
+        load.wait()
+    for load in loads[4:9]:
         load.start()
 
-    def pick(n, carry):
-        f = n // 16
-        k = lax.rem(n, 16) * 32
-        for i in range(32):
-            r = touched_s[f, k + i]
-            trows[f, pl.ds(k + i, 1), :] = table_v[f, pl.ds(r, 1), :]
-        return carry
-
-    lax.fori_loop(0, 64, pick, 0)
+    for f in range(4):
+
+        def pick(n, carry):
+            k = pl.multiple_of(n * 32, 32)
+            for i in range(32):
+                r = touched_s[f * 512 + k + i]
+                trows[f, pl.ds(k + i, 1), :] = table_v[f, pl.ds(r, 1), :]
+            return carry
+
+        lax.fori_loop(0, 16, pick, 0)
     for f in range(4):
         ttr[c * 4 + f, 0:128, :] = (trows[f] * scale).T.astype(BF)
     trade(2).start()
+    loads[4].wait()
+
+    def project(f):
+        side = w_v[p * 8 + f].astype(F32).T.astype(BF)
+        ttr[f, 128:256, :] = split_dot(side, ttr[f, 0:128, :], ((1,), (0,))).astype(BF)
+
     traded(0).wait_recv()
     traded(1).wait_recv()
     lax.fori_loop(0, 4, early_other, 0)
-    loads[4].wait()
     traded(2).wait_recv()
-    for f in range(8):
-        side = w_v[p * 8 + f].astype(F32).T.astype(BF)
-        ttr[f, 128:256, :] = split_dot(side, ttr[f, 0:128, :], ((1,), (0,))).astype(BF)
+    for f in range(4):
+        project(f)
+        project(4 + f)
 
     rows8 = lax.broadcasted_iota(jnp.int32, (8, 256), 0)
 
@@ -557,7 +576,11 @@
         pltpu.make_async_copy(source, target, sem.at[i])
         for i, (source, target) in enumerate(
             (
-                (touched_h, touched_s), (accum_h, accum), (macc_h, macc),
+                (touched_h.at[0], touched_s.at[pl.ds(0, 512)]),
+                (touched_h.at[1], touched_s.at[pl.ds(512, 512)]),
+                (touched_h.at[2], touched_s.at[pl.ds(1024, 512)]),
+                (touched_h.at[3], touched_s.at[pl.ds(1536, 512)]),
+                (accum_h, accum), (macc_h, macc),
                 (dense_h, dense), (noise_h, noise),
             )
         )
@@ -567,29 +590,31 @@
     for f in range(1, 4):
         load(f).start()
         load_rows(f).start()
-    for copy in small:
+    for copy in small[:4]:
+        copy.wait()
+    for f in range(4):
+        load(f).wait()
+        load_rows(f).wait()
+
+        def put(n, carry):
+            k = pl.multiple_of(n * 64, 64)
+            for i in range(64):
+                block[f, pl.ds(touched_s[f * 512 + k + i], 1), :] = rows[f, pl.ds(k + i, 1), :]
+            return carry
+
+        lax.fori_loop(0, 8, put, 0)
+        save(f).start()
+    for copy in small[4:]:
         copy.wait()
     dense[...] += noise[...]
-    save_dense = pltpu.make_async_copy(dense, dense_out, sem.at[5])
+    save_dense = pltpu.make_async_copy(dense, dense_out, sem.at[8])
     save_dense.start()
     for f in range(4):
         for q in range(16):
             lanes = slice(q * 128, (q + 1) * 128)
             accum[f : f + 1, lanes] += macc[f, q : q + 1, :]
-    save_accum = pltpu.make_async_copy(accum, accum_out, sem.at[6])
+    save_accum = pltpu.make_async_copy(accum, accum_out, sem.at[9])
     save_accum.start()
-    for f in range(4):
-        load(f).wait()
-        load_rows(f).wait()
-
-        def put(n, carry):
-            k = pl.multiple_of(n * 64, 64)
-            for i in range(64):
-                block[f, pl.ds(touched_s[f, k + i], 1), :] = rows[f, pl.ds(k + i, 1), :]
-            return carry
-
-        lax.fori_loop(0, 8, put, 0)
-        save(f).start()
     save_dense.wait()
     save_accum.wait()
     for f in range(4):
@@ -609,7 +634,7 @@
         in_specs=[hbm] * 8,
         out_specs=(hbm, hbm, hbm),
         scratch_shapes=[
-            pltpu.SMEM((4, 512), jnp.int32),
+            pltpu.SMEM((2048,), jnp.int32),
             pltpu.VMEM((4, 512), jnp.int32),
             pltpu.VMEM((4, 2048), F32),
             pltpu.VMEM((4, 8, 4096), jnp.int32),
@@ -623,7 +648,7 @@
             pltpu.VMEM((128, 128, 128), BF),
             pltpu.VMEM((4, 512, 128), F32),
             pltpu.VMEM((8, 256, 512), BF),
-            pltpu.VMEM((8, 16, 128), jnp.int32),
+            pltpu.VMEM((8, 8, 128), jnp.int32),
             pltpu.VMEM((4, 512, 128), jnp.int32),
             pltpu.VMEM((8, 512, 2048), BF),
             pltpu.VMEM((8, 512, 256), BF),
@@ -642,7 +667,7 @@
             pltpu.VMEM((4, 512, 128), BF),
             pltpu.VMEM((4, 512, 128), BF),
             pltpu.VMEM((4, 32, 128), F32),
-            dma((9,)),
+            dma((12,)),
             dma((3,)), dma((3,)), dma((16,)), dma((16,)), dma((16,)), dma((16,)),
             dma((8,)), dma((8,)),
             dma((6,)), dma((8,)), dma((6,)), dma((8,)), dma((3,)), dma((4,)),
@@ -669,14 +694,14 @@
         in_specs=[hbm] * 7,
         out_specs=(hbm, hbm, hbm),
         scratch_shapes=[
-            pltpu.SMEM((4, 512), jnp.int32),
+            pltpu.SMEM((2048,), jnp.int32),
             pltpu.VMEM((4, 2048), F32),
             pltpu.VMEM((4, 16, 128), F32),
             pltpu.VMEM((4, 32, 128), F32),
             pltpu.VMEM((4, 32, 128), F32),
             pltpu.VMEM((4, 2048, 128), F32),
             pltpu.VMEM((4, 512, 128), F32),
-            dma((7,)), dma((4,)), dma((4,)), dma((4,)),
+            dma((10,)), dma((4,)), dma((4,)), dma((4,)),
         ],
         compiler_params=pltpu.CompilerParams(vmem_limit_bytes=60 * 1024 * 1024),
         name="write_rows",

time: 72 us -> 64.6 us (0.90)
  Pallas kernels: 71.1 us -> 63.8 us
    pallas_call x1, Pallas kernels: 63.5 us -> 59.6 us  [body(): pl.pallas_call(core, out_shape=(jax.ShapeDtypeStruct((4, 512, 128), F32),...]
    pallas_call x1, Pallas kernels: 7.59 us -> 4.19 us  [body(): pl.pallas_call(write_rows, out_shape=(jax.ShapeDtypeStruct((4, 2048, 128)...]
where the time goes in v6:
time: 64.6 us; the launch traced here: 64.4 us
  Pallas kernels  63.8 us (99%)
    pallas_call x1, Pallas kernels, body(): pl.pallas_call(core, out_shape=(jax.ShapeDtypeStruct((4, 512, 128), F32),...  59.6 us
    pallas_call x1, Pallas kernels, body(): pl.pallas_call(write_rows, out_shape=(jax.ShapeDtypeStruct((4, 2048, 128)...  4.19 us

profile of v6, /device:TPU:0, one launch (start us, length us, event | category | flops | bytes accessed | tf_op | source)
XLA Modules:
  0.0 64.4 jit_solution(3392396748309838716)
XLA Ops:
  0.6 59.6 %step.1 = (f32[4,512,128]{2,1,0:T(8,128)}, f32[4,16,128]{2,1,0:T(8,128)}, f32[4,32,128]{2,1,0:T(8,128)}) custom-call(s32[4,512]{1,0:T(4,128)} %touched_h.3, f32[4,2048]{1,0:T(4,128)} %accum_h.3, s32[4,8,4096]{2,1,0:T(8,128)} %ids_h.1, f32[1,128]{1,0:T(1,128)} %bitcast.2, f32[1,128]{1,0:T(1,128)} %bitcast.3, f32[4,512,128]{2,1,0:T(8,128)} %noise_h.2, ...), custom_call_target="tpu_custom_call" | custom-call | flops 6000000000 | bytes 12582912 | tf_op jit(solution)/shard_map/step/pallas_call | solution.py:627
  60.2 4.2 %write_rows.1 = (f32[4,2048,128]{2,1,0:T(8,128)}, f32[4,2048]{1,0:T(4,128)}, f32[4,32,128]{2,1,0:T(8,128)}) custom-call(s32[4,512]{1,0:T(4,128)} %touched_h.3, f32[4,2048]{1,0:T(4,128)} %accum_h.3, f32[4,16,128]{2,1,0:T(8,128)} %get-tuple-element.6.macc_h, f32[4,32,128]{2,1,0:T(8,128)} %get-tuple-element.7.dense_h, f32[4,32,128]{2,1,0:T(8,128)} %noise_h.3, ...), custom_call_target="tpu_custom_call" | custom-call | tf_op jit(solution)/shard_map/write_rows/pallas_call | solution.py:687

commit v7 on v6

--- a/solution.py
+++ b/solution.py
@@ -189,15 +189,8 @@
         ring[f] = block
         counts[f, :, pl.ds(b0, 256)] = block
 
-    def early(n, carry):
+    for n in range(4):
         count(0, c * 4 + n)
-        return carry
-
-    def early_other(n, carry):
-        count(0, 4 - c * 4 + n)
-        return carry
-
-    lax.fori_loop(0, 4, early, 0)
     pl.semaphore_wait(barrier, 19)
     trade(0).start()
     trade(1).start()
@@ -211,13 +204,13 @@
     for f in range(4):
 
         def pick(n, carry):
-            k = pl.multiple_of(n * 32, 32)
-            for i in range(32):
+            k = pl.multiple_of(n * 128, 128)
+            for i in range(128):
                 r = touched_s[f * 512 + k + i]
                 trows[f, pl.ds(k + i, 1), :] = table_v[f, pl.ds(r, 1), :]
             return carry
 
-        lax.fori_loop(0, 16, pick, 0)
+        lax.fori_loop(0, 4, pick, 0)
     for f in range(4):
         ttr[c * 4 + f, 0:128, :] = (trows[f] * scale).T.astype(BF)
     trade(2).start()
@@ -229,7 +222,8 @@
 
     traded(0).wait_recv()
     traded(1).wait_recv()
-    lax.fori_loop(0, 4, early_other, 0)
+    for n in range(4):
+        count(0, 4 - c * 4 + n)
     traded(2).wait_recv()
     for f in range(4):
         project(f)
@@ -352,7 +346,7 @@
         return lax.shift_right_logical(jnp.int32(packed), 4 * n) & 15
 
     def offsets(n):
-        return nth((0, 3, 12, 15, 13, 8, 9, 11), n), nth((1, 4, 5, 7, 2, 6, 14, 10), n)
+        return nth((0, 3, 12, 8, 15, 13, 14, 11), n), nth((1, 4, 2, 5, 7, 6, 9, 10), n)
 
     def clip_copy(off, src):
         return pltpu.make_async_remote_copy(
@@ -417,6 +411,9 @@
     arrived(1)
     lax.fori_loop(1, 8, gather, 0)
 
+    def turn(i):
+        return (2, 1, 3, 0)[i]
+
     def piece(part):
         return pl.ds(part * 256, 256)
 
@@ -431,25 +428,25 @@
         return pltpu.make_async_remote_copy(
             src_ref=zsend.at[i, piece(part)], dst_ref=zrecv.at[src, piece(part)],
             send_sem=s5.at[part * 3 + i], recv_sem=r5.at[part * 4 + src],
-            device_id=(lax.rem(g + 1 + i, 4), t), device_id_type=MESH,
+            device_id=(lax.rem(g + turn(i), 4), t), device_id_type=MESH,
         )
 
     def row_copy(part, i, src):
         return pltpu.make_async_remote_copy(
             src_ref=rg.at[src, piece(part)], dst_ref=rg.at[src, piece(part)],
             send_sem=s6.at[part * 3 + i], recv_sem=r6.at[part * 4 + src],
-            device_id=(lax.rem(g + 1 + i, 4), t), device_id_type=MESH,
+            device_id=(lax.rem(g + turn(i), 4), t), device_id_type=MESH,
         )
 
     def dense_copy(i, src):
-        to = lax.rem(g + 1 + i, 4)
+        to = lax.rem(g + turn(i), 4)
         return pltpu.make_async_remote_copy(
             src_ref=dsend.at[to], dst_ref=dense_v.at[src], send_sem=s7.at[i],
             recv_sem=r7.at[src], device_id=(to, t), device_id_type=MESH,
         )
 
     def source(i):
-        return lax.rem(g + 3 - i, 4)
+        return lax.rem(g + 4 - turn(i), 4)
 
     def rows_sum(f, part):
         rows = slice(part * 256, part * 256 + 256)
@@ -457,31 +454,25 @@
 
     for part in range(2):
 
-        def other_features(i, carry):
-            f = 4 - c * 4 + lax.rem(g + 1 + i, 4)
+        for i in range(4):
+            f = 4 - c * 4 + lax.rem(g + turn(i), 4)
             half_send[i, piece(part)] = rows_sum(f, part).astype(BF)
+        for i in range(4):
             half_copy(part, i).start()
-            return carry
-
-        lax.fori_loop(0, 4, other_features, 0)
 
     for part in range(2):
-
-        def own_features(i, carry):
-            f = c * 4 + lax.rem(g + 1 + i, 4)
-            total = rows_sum(f, part)
+        for i in range(4):
+            f = c * 4 + lax.rem(g + turn(i), 4)
+            s_acc[f, piece(part)] = rows_sum(f, part)
+        for i in range(4):
+            f = c * 4 + lax.rem(g + turn(i), 4)
             half_copy(part, i).wait_recv()
-            total = total + half_recv[i, piece(part)].astype(F32)
-            s_acc[f, piece(part)] = total
-
-            @pl.when(i < 3)
-            def _():
+            total = s_acc[f, piece(part)] + half_recv[i, piece(part)].astype(F32)
+            if i < 3:
                 zsend[i, piece(part)] = total.astype(BF)
                 sum_copy(part, i, g).start()
-
-            return carry
-
-        lax.fori_loop(0, 4, own_features, 0)
+            else:
+                s_acc[f, piece(part)] = total
 
     def drain_far(off, carry):
         clip_copy(off, p).wait_send()
@@ -597,12 +588,12 @@
         load_rows(f).wait()
 
         def put(n, carry):
-            k = pl.multiple_of(n * 64, 64)
-            for i in range(64):
+            k = pl.multiple_of(n * 128, 128)
+            for i in range(128):
                 block[f, pl.ds(touched_s[f * 512 + k + i], 1), :] = rows[f, pl.ds(k + i, 1), :]
             return carry
 
-        lax.fori_loop(0, 8, put, 0)
+        lax.fori_loop(0, 4, put, 0)
         save(f).start()
     for copy in small[4:]:
         copy.wait()

time: 64.6 us -> 64 us (level); the launches traced: 64.4 us -> 62.8 us
  Pallas kernels: 63.8 us -> 62.2 us
    pallas_call x1, Pallas kernels: 59.6 us -> 58 us  [body(): pl.pallas_call(core, out_shape=(jax.ShapeDtypeStruct((4, 512, 128), F32),...]
where the time goes in v7:
time: 64 us; the launch traced here: 62.8 us
  Pallas kernels  62.2 us (97%)
  between operations  0.64 us (1%)
    pallas_call x1, Pallas kernels, body(): pl.pallas_call(core, out_shape=(jax.ShapeDtypeStruct((4, 512, 128), F32),...  58 us
    pallas_call x1, Pallas kernels, body(): pl.pallas_call(write_rows, out_shape=(jax.ShapeDtypeStruct((4, 2048, 128)...  4.14 us

profile of v7, /device:TPU:0, one launch (start us, length us, event | category | flops | bytes accessed | tf_op | source)
XLA Modules:
  0.0 62.8 jit_solution(2947971992838792749)
XLA Ops:
  0.6 58.0 %step.1 = (f32[4,512,128]{2,1,0:T(8,128)}, f32[4,16,128]{2,1,0:T(8,128)}, f32[4,32,128]{2,1,0:T(8,128)}) custom-call(s32[4,512]{1,0:T(4,128)} %touched_h.3, f32[4,2048]{1,0:T(4,128)} %accum_h.3, s32[4,8,4096]{2,1,0:T(8,128)} %ids_h.1, f32[1,128]{1,0:T(1,128)} %bitcast.2, f32[1,128]{1,0:T(1,128)} %bitcast.3, f32[4,512,128]{2,1,0:T(8,128)} %noise_h.2, ...), custom_call_target="tpu_custom_call" | custom-call | flops 6000000000 | bytes 12582912 | tf_op jit(solution)/shard_map/step/pallas_call | solution.py:618
  58.7 4.1 %write_rows.1 = (f32[4,2048,128]{2,1,0:T(8,128)}, f32[4,2048]{1,0:T(4,128)}, f32[4,32,128]{2,1,0:T(8,128)}) custom-call(s32[4,512]{1,0:T(4,128)} %touched_h.3, f32[4,2048]{1,0:T(4,128)} %accum_h.3, f32[4,16,128]{2,1,0:T(8,128)} %get-tuple-element.6.macc_h, f32[4,32,128]{2,1,0:T(8,128)} %get-tuple-element.7.dense_h, f32[4,32,128]{2,1,0:T(8,128)} %noise_h.3, ...), custom_call_target="tpu_custom_call" | custom-call | tf_op jit(solution)/shard_map/write_rows/pallas_call | solution.py:678

commit v8 on v7

--- a/solution.py
+++ b/solution.py
@@ -271,6 +271,32 @@
     for f in range(8):
         s_acc[f] = jnp.zeros((512, 128), F32)
 
+    def high_one(f):
+        row = lax.shift_right_logical(touched_v[pl.ds(f, 1), :], 7)
+        return jnp.where(high_of == row, 1.0, 0.0).astype(BF)
+
+    def three(values):
+        first = values.astype(BF)
+        rest = values - first.astype(F32)
+        second = rest.astype(BF)
+        return first, second, (rest - second.astype(F32)).astype(BF)
+
+    lanes = lax.broadcasted_iota(jnp.int32, (512, 128), 1)
+    loads[8].wait()
+    for f in range(4):
+        is_high = high_one(f)
+        values = jnp.concatenate(
+            [accum[f : f + 1, q * 128 : (q + 1) * 128] for q in range(16)], axis=0
+        )
+        first, second, third = three(values)
+        spread_out = split_dot(
+            jnp.concatenate([is_high, is_high, is_high], axis=0),
+            jnp.concatenate([first, second, third], axis=0),
+            ((0,), (0,)),
+        )
+        found = jnp.where(lanes == low_col[f], spread_out, 0.0)
+        accb[f] = jnp.broadcast_to(jnp.sum(found, axis=1, keepdims=True), (512, 128))
+
     pacc[...] = slots[p, 0:128, :].astype(F32)
 
     def from_chip(src):
@@ -330,16 +356,6 @@
     factor = CLIP / jnp.maximum(jnp.sqrt(norm_sq), CLIP)
     clip[p] = (factor * delta).T.astype(BF)
 
-    def high_one(f):
-        row = lax.shift_right_logical(touched_v[pl.ds(f, 1), :], 7)
-        return jnp.where(high_of == row, 1.0, 0.0).astype(BF)
-
-    def three(values):
-        first = values.astype(BF)
-        rest = values - first.astype(F32)
-        second = rest.astype(BF)
-        return first, second, (rest - second.astype(F32)).astype(BF)
-
     def nth(table, n):
         packed = sum(v << (4 * i) for i, v in enumerate(table))
         packed = packed - (1 << 32) if packed >= 1 << 31 else packed
@@ -361,22 +377,6 @@
 
     clip_copy(1, p).start()
     lax.fori_loop(1, 8, spread, 0)
-
-    lanes = lax.broadcasted_iota(jnp.int32, (512, 128), 1)
-    loads[8].wait()
-    for f in range(4):
-        is_high = high_one(f)
-        values = jnp.concatenate(
-            [accum[f : f + 1, q * 128 : (q + 1) * 128] for q in range(16)], axis=0
-        )
-        first, second, third = three(values)
-        spread_out = split_dot(
-            jnp.concatenate([is_high, is_high, is_high], axis=0),
-            jnp.concatenate([first, second, third], axis=0),
-            ((0,), (0,)),
-        )
-        found = jnp.where(lanes == low_col[f], spread_out, 0.0)
-        accb[f] = jnp.broadcast_to(jnp.sum(found, axis=1, keepdims=True), (512, 128))
 
     def product(f, n, first=0, rows=512):
         chips = [behind(off) for off in offsets(n)]
@@ -390,16 +390,6 @@
 
     def arrived(off):
         clip_copy(off, behind(off)).wait_recv()
-
-    def drain(s, carry):
-        out_copy(s, 0).wait_send()
-        out_copy(s, 1).wait_send()
-        return carry
-
-    lax.fori_loop(0, 7, drain, 0)
-    out_copy(7, 1 - odd).wait_send()
-    for i in range(3):
-        trade(i).wait_send()
 
     def gather(n, carry):
         for f in range(8):
@@ -473,6 +463,16 @@
                 sum_copy(part, i, g).start()
             else:
                 s_acc[f, piece(part)] = total
+
+    def drain(s, carry):
+        out_copy(s, 0).wait_send()
+        out_copy(s, 1).wait_send()
+        return carry
+
+    lax.fori_loop(0, 7, drain, 0)
+    out_copy(7, 1 - odd).wait_send()
+    for i in range(3):
+        trade(i).wait_send()
 
     def drain_far(off, carry):
         clip_copy(off, p).wait_send()

time: 64 us -> 64 us (level)
  no operation moved by 1% of the time
where the time goes in v8:
time: 64 us; the launch traced here: 62.8 us
  Pallas kernels  62.2 us (97%)
  between operations  0.64 us (1%)
    pallas_call x1, Pallas kernels, body(): pl.pallas_call(core, out_shape=(jax.ShapeDtypeStruct((4, 512, 128), F32),...  58 us
    pallas_call x1, Pallas kernels, body(): pl.pallas_call(write_rows, out_shape=(jax.ShapeDtypeStruct((4, 2048, 128)...  4.14 us

profile of v8, /device:TPU:0, one launch (start us, length us, event | category | flops | bytes accessed | tf_op | source)
XLA Modules:
  0.0 62.8 jit_solution(16022987640027021603)
XLA Ops:
  0.6 58.0 %step.1 = (f32[4,512,128]{2,1,0:T(8,128)}, f32[4,16,128]{2,1,0:T(8,128)}, f32[4,32,128]{2,1,0:T(8,128)}) custom-call(s32[4,512]{1,0:T(4,128)} %touched_h.3, f32[4,2048]{1,0:T(4,128)} %accum_h.3, s32[4,8,4096]{2,1,0:T(8,128)} %ids_h.1, f32[1,128]{1,0:T(1,128)} %bitcast.2, f32[1,128]{1,0:T(1,128)} %bitcast.3, f32[4,512,128]{2,1,0:T(8,128)} %noise_h.2, ...), custom_call_target="tpu_custom_call" | custom-call | flops 6000000000 | bytes 12582912 | tf_op jit(solution)/shard_map/step/pallas_call | solution.py:618
  58.7 4.1 %write_rows.1 = (f32[4,2048,128]{2,1,0:T(8,128)}, f32[4,2048]{1,0:T(4,128)}, f32[4,32,128]{2,1,0:T(8,128)}) custom-call(s32[4,512]{1,0:T(4,128)} %touched_h.3, f32[4,2048]{1,0:T(4,128)} %accum_h.3, f32[4,16,128]{2,1,0:T(8,128)} %get-tuple-element.6.macc_h, f32[4,32,128]{2,1,0:T(8,128)} %get-tuple-element.7.dense_h, f32[4,32,128]{2,1,0:T(8,128)} %noise_h.3, ...), custom_call_target="tpu_custom_call" | custom-call | tf_op jit(solution)/shard_map/write_rows/pallas_call | solution.py:678
